TPU v7x, 32 devices: a whole 2x2x4 slice. The times are simulated.
32 devices in a mesh: dp: 8 (over z, y), fsdp: 4 (over x, core).
Axes of the slice: x: 2, y: 2, z: 4, core: 2. Of those that a mesh axis runs over, the one named last changes fastest.
Arguments:
- inputs: bfloat16 [32768, 512], P(('dp', 'fsdp')), may hold values from -6 to 6
- memory: bfloat16 [65536, 512], P(('dp', 'fsdp')), may hold values from -6 to 6
- seg_lengths: int32 [32, 16], P(('dp', 'fsdp')), may hold values from 1 to 256, 1024 in all within a row
- mem_lengths: int32 [32, 17], P(('dp', 'fsdp')), may hold values from 1 to 256, 2048 in all within a row
- self_query: bfloat16 [262144], P(('dp', 'fsdp')), may hold values from -0.25 to 0.25
- self_key: bfloat16 [262144], P(('dp', 'fsdp')), may hold values from -0.25 to 0.25
- self_value: bfloat16 [262144], P(('dp', 'fsdp')), may hold values from -0.25 to 0.25
- self_out: bfloat16 [262144], P(('dp', 'fsdp')), may hold values from -1 to 1
- cross_query: bfloat16 [262144], P(('dp', 'fsdp')), may hold values from -0.25 to 0.25
- cross_key: bfloat16 [262144], P(('dp', 'fsdp')), may hold values from -0.25 to 0.25
- cross_value: bfloat16 [262144], P(('dp', 'fsdp')), may hold values from -0.25 to 0.25
- cross_out: bfloat16 [262144], P(('dp', 'fsdp')), may hold values from -1 to 1
- ffn_in: bfloat16 [1048576], P(('dp', 'fsdp')), may hold values from -0.25 to 0.25
- ffn_out: bfloat16 [1048576], P(('dp', 'fsdp')), may hold values from -0.125 to 0.125
- norm_params: float32 [3072], P(('dp', 'fsdp')), may hold values from -1.2 to 1.45
- cotangent: bfloat16 [32768, 512], P(('dp', 'fsdp')), may hold values from -6 to 6
Outputs:
- block_output: bfloat16 [32768, 512], P(('dp', 'fsdp'))
- grad_inputs: bfloat16 [32768, 512], P(('dp', 'fsdp'))
- grad_memory: bfloat16 [65536, 512], P(('dp', 'fsdp'))
- grad_self_query: float32 [262144], P(('dp', 'fsdp'))
- grad_self_key: float32 [262144], P(('dp', 'fsdp'))
- grad_self_value: float32 [262144], P(('dp', 'fsdp'))
- grad_self_out: float32 [262144], P(('dp', 'fsdp'))
- grad_cross_query: float32 [262144], P(('dp', 'fsdp'))
- grad_cross_key: float32 [262144], P(('dp', 'fsdp'))
- grad_cross_value: float32 [262144], P(('dp', 'fsdp'))
- grad_cross_out: float32 [262144], P(('dp', 'fsdp'))
- grad_ffn_in: float32 [1048576], P(('dp', 'fsdp'))
- grad_ffn_out: float32 [1048576], P(('dp', 'fsdp'))
- grad_norm_params: float32 [3072], P(('dp', 'fsdp'))
Inputs may be any that keep to these rules, and one draw needn't show every extreme that they name: `seg_lengths`: each row sums to 1024. `mem_lengths`: each row sums to 2048; the last entry counts padding rows at the end of the stream's memory.
All inputs are finite; a program needn't handle non-finite values.
Results may differ from a plain program's by a relative error of at most 0.03.
Values may be sent and summed in bfloat16 or wider, within the bound.
No kernel may reach another device: no remote copies, remote signals or barrier semaphores. Data moves between devices by JAX's collectives and lax.ppermute only.
A program may use at most 256 MiB of HBM per device.

v0:
```python
import functools
import jax
import jax.numpy as jnp
from jax import lax
from jax.experimental import pallas as pl
from jax.experimental.pallas import tpu as pltpu
from jax.sharding import PartitionSpec as P

HD = 64
LANES = 128
MOST = 256
QROWS = 128
EACH = (2, 4)
PADDING = 4
FFN_CHUNK = 256
masked_score = -1e30
norm_eps = 1e-05
bf16, f32 = jnp.bfloat16, jnp.float32
NT = (((1,), (1,)), ((), ()))
TN = (((0,), (0,)), ((), ()))
NN = (((1,), (0,)), ((), ()))


def mm(left, right, dims=NN):
    return lax.dot_general(left, right, dims, preferred_element_type=f32)


def norm_rows(source):
    mean = jnp.mean(source, axis=-1, keepdims=True)
    centered = source - mean
    variance = jnp.mean(centered * centered, axis=-1, keepdims=True)
    rstd = lax.rsqrt(variance + norm_eps)
    return centered * rstd, rstd


def lane_below(rows):
    return lax.broadcasted_iota(jnp.int32, (rows, LANES), 1) < HD


def column_of(row):
    return jnp.broadcast_to(row, (LANES, row.shape[1])).T


def head_part(pair, which, low):
    return jnp.where(low == (which == 0), pair, jnp.zeros_like(pair))


def values_with_ones(values):
    parts = []
    for p in range(values.shape[1] // LANES):
        pair = values[:, p * LANES : (p + 1) * LANES]
        parts += [pair, jnp.ones_like(pair)]
    return jnp.concatenate(parts, axis=1)


def finish_heads(at, top, tot, acc, write):
    shape = acc.shape[0], at.size if hasattr(at, "size") else at.stop - at.start, LANES
    lane = lax.broadcasted_iota(jnp.int32, shape[1:], 1)
    sums, tops = jnp.ones(shape[1:], f32), jnp.zeros(shape[1:], f32)
    for p in range(shape[0]):
        total = tot[p, at, :]
        write(p, (acc[p, at, :] / total).astype(bf16))
        sums = jnp.where(lane % HD == p, total, sums)
        tops = jnp.where(lane == p, top[2 * p, at, :], jnp.where(lane == HD + p, top[2 * p + 1, at, :], tops))
    return tops + jnp.log(sums)


def column_at(head):
    return head % 2 * HD + head // 2


def item_at(items_ref, n, idk_ref, ids_q, keys, tile, block, causal):
    begin = pl.multiple_of(items_ref[0, n] * block, block)
    wanted = items_ref[1, n] * LANES
    start = pl.multiple_of(jnp.minimum(wanted, keys - tile), LANES)
    at = pl.ds(begin, block)
    pos = start + lax.broadcasted_iota(jnp.int32, (1, tile), 1)
    ids_k = jnp.where(pos >= wanted, idk_ref[:, pl.ds(start, tile)], -1)
    allowed = ids_q[at, :1] == ids_k
    if causal:
        allowed &= pos <= begin + lax.broadcasted_iota(jnp.int32, (block, 1), 0)
    return at, pl.ds(start, tile), jnp.where(allowed, 0.0, masked_score).astype(f32)


def attend(items_ref, idk_ref, ids_q, q_all, k_all, vx_all, top, tot, acc, tile, block, causal):
    keys, width = k_all.shape
    pairs = width // LANES
    heads = 2 * pairs
    low = lane_below(block)
    top[...] = jnp.full(top.shape, masked_score, f32)
    tot[...] = jnp.zeros(tot.shape, f32)
    acc[...] = jnp.zeros(acc.shape, f32)

    def some(i, _):
        loads, made = [], []
        for t in range(EACH[0]):
            at, there, bias = item_at(items_ref, EACH[0] * i + t, idk_ref, ids_q, keys, tile, block, causal)
            loads.append((at, there, bias))
            for p in range(pairs):
                cols = slice(p * LANES, (p + 1) * LANES)
                part = q_all[at, cols]
                both = jnp.concatenate([head_part(part, h, low) for h in range(2)])
                made.append(mm(both, k_all[there, cols], NT))
        weights, scales = [], []
        for t, (at, there, bias) in enumerate(loads):
            for head in range(heads):
                s = made[t * pairs + head // 2][head % 2 * block : (head % 2 + 1) * block] + bias
                old = top[head, at, :]
                new = jnp.maximum(old, jnp.max(s, axis=1, keepdims=True))
                top[head, at, :] = new
                scales.append(jnp.exp(old - new))
                weights.append(jnp.exp(s - jnp.concatenate([new] * (tile // LANES), axis=1)).astype(bf16))
        mixed = [
            mm(jnp.concatenate(weights[t * heads + 2 * p : t * heads + 2 * p + 2]), vx_all[there, 2 * p * LANES : 2 * (p + 1) * LANES])
            for t, (_, there, _) in enumerate(loads) for p in range(pairs)
        ]
        for t, (at, _, _) in enumerate(loads):
            for p in range(pairs):
                n = t * pairs + p
                scale = jnp.where(low, scales[2 * n], scales[2 * n + 1])
                o = mixed[n]
                acc[p, at, :] = acc[p, at, :] * scale + jnp.where(low, o[:block, :LANES], o[block:, :LANES])
                tot[p, at, :] = tot[p, at, :] * scale + jnp.where(low, o[:block, LANES:], o[block:, LANES:])
        return 0

    lax.fori_loop(0, items_ref[2, 0], some, 0)


def attend_back(items_ref, idk_ref, ids_q, q_all, do_ref, k_ref, v_ref, l_ref, delta_ref, dq, dk, dv, tile, block, first_head, causal, each):
    keys, width = k_ref.shape
    pairs = width // LANES
    low = lane_below(block)

    def some(i, _):
        loads, scores, grads = [], [], []
        for t in range(each):
            at, there, bias = item_at(items_ref, each * i + t, idk_ref, ids_q, keys, tile, block, causal)
            loads.append((at, there, bias))
            for p in range(pairs):
                cols = slice(p * LANES, (p + 1) * LANES)
                q, do = q_all[at, cols], do_ref[at, cols]
                qs = jnp.concatenate([head_part(q, h, low) for h in range(2)])
                dos = jnp.concatenate([head_part(do, h, low) for h in range(2)])
                scores.append((mm(qs, k_ref[there, cols], NT), qs))
                grads.append((mm(dos, v_ref[there, cols], NT), dos))
        weights, slopes = [], []
        for t, (at, there, bias) in enumerate(loads):
            logs, deltas = l_ref[at, :], delta_ref[at, :]
            for p in range(pairs):
                es, ds = [], []
                for h in range(2):
                    lane = column_at(first_head + 2 * p + h)
                    rows = slice(h * block, (h + 1) * block)
                    e = jnp.exp(scores[t * pairs + p][0][rows] + bias - logs[:, lane : lane + 1])
                    es.append(e.astype(bf16))
                    ds.append((e * (grads[t * pairs + p][0][rows] - deltas[:, lane : lane + 1])).astype(bf16))
                weights.append(jnp.concatenate(es))
                slopes.append(jnp.concatenate(ds))
        for t, (at, there, _) in enumerate(loads):
            for p in range(pairs):
                cols = slice(p * LANES, (p + 1) * LANES)
                n = t * pairs + p
                gq = mm(slopes[n], k_ref[there, cols])
                gk = mm(slopes[n], scores[n][1], TN)
                gv = mm(weights[n], grads[n][1], TN)
                dq[at, cols] += jnp.where(low, gq[:block], gq[block:])
                dk[there, cols] += gk
                dv[there, cols] += gv
        return 0

    lax.fori_loop(0, items_ref[2, EACH.index(each)], some, 0)


def self_forward_kernel(tile, block, items_ref, x_ref, wq_ref, wk_ref, wv_ref, idr_ref, *rest):
    q_ref, k_ref, v_ref, o_ref, l_ref, q_all, k_all, vx_all, ids_all, top, tot, acc = rest[-12:]
    step = pl.program_id(0)
    rows = x_ref.shape[0]
    total, width = k_all.shape
    turns = total // rows

    @pl.when(step < turns)
    def _():
        x = x_ref[...]
        q = mm(x, wq_ref[0]).astype(bf16)
        k = mm(x, wk_ref[0]).astype(bf16)
        v = mm(x, wv_ref[0]).astype(bf16)
        q_ref[...] = q
        k_ref[...] = k
        v_ref[...] = v
        here = pl.ds(pl.multiple_of(step * rows, rows), rows)
        q_all[here, :] = q * jnp.asarray(HD ** -0.5, bf16)
        k_all[here, :] = k
        vx_all[here, :] = values_with_ones(v)
        ids_all[here, :] = column_of(idr_ref[:, here])

    @pl.when(step == turns)
    def _():
        attend(items_ref, idr_ref, ids_all, q_all, k_all, vx_all, top, tot, acc, tile, block, True)
        size = 2 * block
        for j in range(total // size):
            at = slice(j * size, (j + 1) * size)

            def write(p, value):
                o_ref[at, p * LANES : (p + 1) * LANES] = value

            l_ref[at, :] = finish_heads(at, top, tot, acc, write)


def whole(a):
    return pl.BlockSpec(a.shape, lambda *_: (0,) * a.ndim)


def once(a):
    return pl.BlockSpec(a.shape, lambda *_: (0,) * a.ndim, pipeline_mode=pl.Buffered(1))


def part(weights, index, columns, half):
    return pl.BlockSpec((1, weights.shape[1], columns), lambda *_: (index, 0, half))


def params(us, vmem):
    return dict(
        compiler_params=pltpu.CompilerParams(vmem_limit_bytes=vmem * 2**20),
        cost_estimate=pl.CostEstimate(flops=us * 10**9, bytes_accessed=2**20, transcendentals=0),
    )


apart = pl.BlockSpec(memory_space=pl.ANY)


def out_array(shape, dtype):
    return pltpu.HBM(shape, dtype)


def placed(*arrays):
    return [pltpu.with_memory_space_constraint(a, pltpu.HBM) for a in arrays]


def self_forward(items, x, weights, idr, after, turns=2, block=QROWS, tile=256):
    total, width = x.shape
    heads = width // HD
    rows = total // turns
    early = lambda w: pl.BlockSpec((rows, w), lambda i, *_: (jnp.minimum(i, turns - 1), 0))
    fixed = lambda w: pl.BlockSpec((total, w), lambda i, *_: (0, 0))
    sds = out_array
    full = sds((total, width), bf16)
    return pl.pallas_call(
        functools.partial(self_forward_kernel, tile, block),
        grid_spec=pltpu.PrefetchScalarGridSpec(
            num_scalar_prefetch=1,
            grid=(turns + 1,),
            in_specs=[early(width)] + [part(weights, i, width, 0) for i in range(3)] + [whole(idr)] + [apart] * len(after),
            out_specs=[early(width)] * 3 + [fixed(width), fixed(LANES)],
            scratch_shapes=[
                pltpu.VMEM((total, width), bf16), pltpu.VMEM((total, width), bf16), pltpu.VMEM((total, 2 * width), bf16),
                pltpu.VMEM((total, LANES), jnp.int32),
                pltpu.VMEM((heads, total, LANES), f32), pltpu.VMEM((heads // 2, total, LANES), f32), pltpu.VMEM((heads // 2, total, LANES), f32),
            ],
        ),
        out_shape=[full] * 4 + [sds((total, LANES), f32)],
        name="self_forward",
        **params(13, 32),
    )(items, *placed(x), weights, weights, weights, idr, *after)


def cross_forward_kernel(
    tile, block, items_ref, memory_ref, wk_ref, wv_ref, x_ref, o1_ref, wso_ref, wcq_ref, norms_ref, idr_ref, idk_ref, *rest
):
    k2_ref, v2_ref, r1_ref, h1b_ref, q2_ref, h1_ref, o_ref, l_ref, k_all, vx_all, q_all, ids_all, top, tot, acc = rest[-15:]
    step = pl.program_id(0)
    rows, width = x_ref.shape
    keys = k_all.shape[0]
    turns = pl.num_programs(0) - 1

    @pl.when(step < turns)
    def _():
        per = memory_ref.shape[0]
        memory = memory_ref[...]
        r1 = x_ref[...].astype(f32) + mm(o1_ref[...], wso_ref[0])
        k2 = mm(memory, wk_ref[0]).astype(bf16)
        r1_ref[...] = r1.astype(bf16)
        n1, _ = norm_rows(r1)
        v2 = mm(memory, wv_ref[0]).astype(bf16)
        h1 = n1 * norms_ref[0:1, :] + norms_ref[1:2, :]
        h1b = h1.astype(bf16)
        h1b_ref[...] = h1b
        q2 = mm(h1b, wcq_ref[0]).astype(bf16)
        q2_ref[...] = q2
        k2_ref[...] = k2
        v2_ref[...] = v2
        here = pl.ds(pl.multiple_of(step * rows, rows), rows)
        q_all[here, :] = q2 * jnp.asarray(HD ** -0.5, bf16)
        h1_ref[...] = h1
        ids_all[here, :] = column_of(idr_ref[:, here])
        there = pl.ds(pl.multiple_of(step * per, per), per)
        k_all[there, :] = k2
        vx_all[there, :] = values_with_ones(v2)

    @pl.when(step == turns)
    def _():
        attend(items_ref, idk_ref, ids_all, q_all, k_all, vx_all, top, tot, acc, tile, block, False)

        size = 2 * block
        for j in range(q_all.shape[0] // size):
            at = slice(j * size, (j + 1) * size)

            def write(p, value):
                o_ref[at, p * LANES : (p + 1) * LANES] = value

            l_ref[at, :] = finish_heads(at, top, tot, acc, write)


def cross_forward(items, memory, x, o1, weights, norms, idr, idk, after, turns=2, block=QROWS, tile=256):
    total, width = x.shape
    keys = memory.shape[0]
    heads = width // HD
    rows, per = total // turns, keys // turns
    early = lambda r, w: pl.BlockSpec((r, w), lambda i, *_: (jnp.minimum(i, turns - 1), 0))
    fixed = lambda w: pl.BlockSpec((total, w), lambda i, *_: (0, 0))
    sds = out_array
    return pl.pallas_call(
        functools.partial(cross_forward_kernel, tile, block),
        grid_spec=pltpu.PrefetchScalarGridSpec(
            num_scalar_prefetch=1,
            grid=(turns + 1,),
            in_specs=[early(per, width), part(weights, 2, width, 0), part(weights, 3, width, 0)]
            + [early(rows, width), early(rows, width), part(weights, 0, width, 0), part(weights, 1, width, 0)]
            + [whole(norms), whole(idr), whole(idk)] + [apart] * len(after),
            out_specs=[early(per, width)] * 2 + [early(rows, width)] * 4 + [fixed(width), fixed(LANES)],
            scratch_shapes=[
                pltpu.VMEM((keys, width), bf16),
                pltpu.VMEM((keys, 2 * width), bf16),
                pltpu.VMEM((total, width), bf16),
                pltpu.VMEM((total, LANES), jnp.int32),
                pltpu.VMEM((heads, total, LANES), f32),
                pltpu.VMEM((heads // 2, total, LANES), f32),
                pltpu.VMEM((heads // 2, total, LANES), f32),
            ],
        ),
        out_shape=[
            sds((keys, width), bf16), sds((keys, width), bf16), sds((total, width), bf16), sds((total, width), bf16),
            sds((total, width), bf16), sds((total, width), f32), sds((total, width), bf16), sds((total, LANES), f32),
        ],
        name="cross_forward",
        **params(19, 44),
    )(items, *placed(memory), weights, weights, *placed(x, o1), weights, weights, norms, idr, idk, *after)


def norm_back(incoming, normal, rstd, gain):
    m = incoming * gain
    return rstd * (
        m - jnp.mean(m, axis=-1, keepdims=True) - normal * jnp.mean(m * normal, axis=-1, keepdims=True)
    )


def head_columns(left, right):
    width = left.shape[1]
    prod = left.astype(f32) * right.astype(f32)
    lane = lax.broadcasted_iota(jnp.int32, (width, LANES), 1)
    own = lax.broadcasted_iota(jnp.int32, (width, LANES), 0) // HD == 2 * (lane % HD) + lane // HD
    own = own.astype(bf16)
    high = prod.astype(bf16)
    low = (prod - high.astype(f32)).astype(bf16)
    return mm(high, own) + mm(low, own)


def column_sums(a):
    return jnp.sum(a, axis=0, keepdims=True)


def spread(keep_ref, send_ref, core, write):
    def one(j, _):
        write(2 * j + core, keep_ref, j)
        write(2 * j + 1 - core, send_ref, j)
        return 0

    lax.fori_loop(0, keep_ref.shape[0], one, 0)


def ffn_kernel(
    core_ref, here_ref, h1_ref, x_ref, cot_ref, o2_ref, norms_ref, *rest
):
    count = len(rest) - 11
    pieces = 8 if count >= 8 else 2
    weights, rest = rest[:pieces], rest[pieces:]
    out_ref, dr3_ref, dr2_ref, do2_ref, delta_ref, keep_ref, send_ref, gn_ref, gin, gout, gco = rest[:11]
    wa_ref, wb_ref = rest[11:] if pieces == 8 else weights
    step = pl.program_id(0)
    last = pl.num_programs(0) - 1
    width = x_ref.shape[1]
    share = width // wb_ref.shape[0]
    blocks = wb_ref.shape[1] // share

    @pl.when(step == 0)
    def _():
        if pieces == 8:
            bits = here_ref[0], here_ref[1]
            for n, (ref, axis) in enumerate(((wa_ref, 1), (wb_ref, 0))):
                for m in range(4):
                    across, core = bits[axis] ^ (m % 2), here_ref[2] ^ (m // 2)
                    piece = weights[4 * n + m]
                    for z in range(piece.shape[0]):
                        for other in range(2):
                            planes = (across, other) if axis else (other, across)
                            ref[z * 8 + planes[0] * 4 + planes[1] * 2 + core] = piece[z, other]
        gin[...] = jnp.zeros_like(gin)
        gout[...] = jnp.zeros_like(gout)
        gco[...] = jnp.zeros_like(gco)
        gn_ref[...] = jnp.zeros_like(gn_ref)

    win = [wa_ref[:, c * share : (c + 1) * share].reshape(width, width) for c in range(blocks)]
    wout = wb_ref[...].reshape(blocks * width, width)
    wco = wa_ref[:, blocks * share :].reshape(width, width)
    n2, rstd2 = norm_rows(h1_ref[...] + mm(o2_ref[...], wco))
    h2 = n2 * norms_ref[2:3, :] + norms_ref[3:4, :]
    h2b = h2.astype(bf16)
    chunk = min(FFN_CHUNK, width)
    parts = blocks * width // chunk
    per = width // chunk

    def win_part(c):
        return win[c // per][:, (c % per) * chunk : (c % per + 1) * chunk]

    acts, slopes, hidden = [], [], [mm(h2b, win_part(0))]
    ff = jnp.zeros(h2.shape, f32)
    for c in range(parts):
        if c + 1 < parts:
            hidden.append(mm(h2b, win_part(c + 1)))
        u = hidden[c]
        square = u * u
        t = jnp.tanh(u * (0.7978845608028654 + (0.7978845608028654 * 0.044715) * square))
        half = 0.5 + 0.5 * t
        acts.append((u * half).astype(bf16))
        rise = u * (0.5 * 0.7978845608028654 + (0.5 * 0.7978845608028654 * 3 * 0.044715) * square)
        slopes.append(half + (1.0 - t * t) * rise)
        if c:
            ff += mm(acts[c - 1], wout[(c - 1) * chunk : c * chunk, :])
    ff += mm(acts[-1], wout[(parts - 1) * chunk :, :])
    r3 = h2 + ff + x_ref[...].astype(f32)
    n3, rstd3 = norm_rows(r3)
    gain3 = norms_ref[4:5, :]
    out_ref[...] = (n3 * gain3 + norms_ref[5:6, :]).astype(bf16)
    e = cot_ref[...].astype(f32)
    gn_ref[2:3, :] += column_sums(e * n3)
    gn_ref[3:4, :] += column_sums(e)
    dr3 = norm_back(e, n3, rstd3, gain3)
    dr3_ref[...] = dr3.astype(bf16)
    dfb = dr3.astype(bf16)
    dh2 = dr3
    raw, made = [mm(dfb, wout[:chunk, :], NT)], []
    for c in range(parts + 1):
        if c + 1 < parts:
            raw.append(mm(dfb, wout[(c + 1) * chunk : (c + 2) * chunk, :], NT))
        if c < parts:
            gout[c * chunk : (c + 1) * chunk, :] += mm(acts[c], dfb, TN)
            made.append((raw[c] * slopes[c]).astype(bf16))
        if c:
            gin[:, (c - 1) * chunk : c * chunk] += mm(h2b, made[c - 1], TN)
            dh2 += mm(made[c - 1], win_part(c - 1), NT)
    gn_ref[0:1, :] += column_sums(dh2 * n2)
    gn_ref[1:2, :] += column_sums(dh2)
    dr2 = norm_back(dh2, n2, rstd2, norms_ref[2:3, :])
    da2 = dr2.astype(bf16)
    dr2_ref[...] = da2
    o2 = o2_ref[...]
    gco[...] += mm(o2, da2, TN)
    do2 = mm(da2, wco, NT).astype(bf16)
    do2_ref[...] = do2
    delta_ref[...] = head_columns(do2, o2)

    @pl.when(step == last)
    def _():
        r = keep_ref.shape[2]

        def write(device, ref, j):
            here = pl.ds(pl.multiple_of(device * r, r), r)
            for c in range(blocks):
                ref[j, c] = gin[here, c * width : (c + 1) * width].astype(bf16)
            ref[j, blocks] = gco[here, :].astype(bf16)
            there = pl.ds(pl.multiple_of(device * blocks * r, blocks * r), blocks * r)
            ref[j, blocks + 1 :] = gout[there, :].astype(bf16).reshape(blocks, r, width)

        spread(keep_ref, send_ref, core_ref[0], write)


def ffn(core, here, pairs, h1, x, cot, o2, weights, norms, rows=256):
    total, width = x.shape
    devices = 1 if len(weights) == 2 else 2 * pairs
    blocks = weights[-1].size // width**2 if devices == 1 else 8 * weights[-1].size // (2 * width**2)
    held = [(devices, (blocks + 1) * width // devices, width), (devices, blocks * width // devices, width)]
    rowspec = lambda w: pl.BlockSpec((rows, w), lambda i: (i, 0))
    smem = pl.BlockSpec(memory_space=pltpu.SMEM)
    sds = out_array
    side = jax.ShapeDtypeStruct((pairs, 2 * blocks + 1, width // (2 * pairs), width), bf16)
    return pl.pallas_call(
        ffn_kernel,
        grid=(total // rows,),
        in_specs=[smem, smem] + [rowspec(width)] * 4 + [whole(norms)] + [once(w) for w in weights],
        out_specs=[rowspec(width)] * 4 + [rowspec(LANES), whole(side), whole(side), pl.BlockSpec((4, width), lambda i: (0, 0))],
        out_shape=[
            sds((total, width), bf16), sds((total, width), bf16), sds((total, width), bf16), sds((total, width), bf16),
            sds((total, LANES), f32), side, side, sds((4, width), f32),
        ],
        scratch_shapes=[pltpu.VMEM((width, blocks * width), f32), pltpu.VMEM((blocks * width, width), f32), pltpu.VMEM((width, width), f32)]
        + ([pltpu.VMEM(h, bf16) for h in held] if devices > 1 else []),
        name="ffn",
        **params(32, 56),
    )(core, here, *placed(h1, x, cot, o2), norms, *weights)


def cross_backward_kernel(
    tile, block, first, count, each, items_ref, q2_ref, k2_ref, v2_ref, do_ref, l_ref, delta_ref, idr_ref, idk_ref, memory_ref, *rest
):
    dq_ref, dk_ref, dv_ref, grads_ref, q_all, ids_all, dq, dk, dv, grads = rest[-10:]
    step = pl.program_id(0)
    total = q2_ref.shape[0]
    begin = first * LANES if q2_ref.shape[1] > count * LANES else 0
    cols = slice(begin, begin + count * LANES)

    @pl.when(step == 0)
    def _():
        dq[...] = jnp.zeros_like(dq)
        dk[...] = jnp.zeros_like(dk)
        dv[...] = jnp.zeros_like(dv)
        grads[...] = jnp.zeros_like(grads)
        q_all[...] = q2_ref[:, cols] * jnp.asarray(HD ** -0.5, bf16)
        for j in range(total // block):
            ids_all[j * block : (j + 1) * block, :] = column_of(idr_ref[:, j * block : (j + 1) * block])
        attend_back(
            items_ref, idk_ref, ids_all, q_all, do_ref.at[:, cols], k2_ref.at[:, cols], v2_ref.at[:, cols], l_ref, delta_ref,
            dq, dk, dv, tile, block, 2 * first, False, each,
        )

    memory = memory_ref[...]
    per = memory.shape[0]
    here = pl.ds(pl.multiple_of(step * per, per), per)
    for i, (ref, out_ref) in enumerate(((dk, dk_ref), (dv, dv_ref))):
        grad = ref[here, :].astype(bf16)
        out_ref[...] = grad
        grads[i] += mm(memory, grad, TN)
    rows = dq_ref.shape[0]
    dq_ref[...] = (dq[pl.ds(pl.multiple_of(step * rows, rows), rows), :] * HD ** -0.5).astype(bf16)

    @pl.when(step == pl.num_programs(0) - 1)
    def _():
        grads_ref[...] = grads[...].astype(bf16)


def cross_backward(items, q2, k2, v2, do, l, delta, idr, idk, memory, first, count, each, after, turns=2, block=QROWS, tile=256):
    total, width = q2.shape
    keys = k2.shape[0]
    columns = count * LANES
    alone = first % count == 0
    cols = lambda r: pl.BlockSpec((r, columns if alone else width), lambda i, *_: (0, first // count if alone else 0))
    rowspec = lambda r, w: pl.BlockSpec((r, w), lambda i, *_: (i, 0))
    sds = jax.ShapeDtypeStruct
    grad = sds((2, width, columns), bf16)
    return pl.pallas_call(
        functools.partial(cross_backward_kernel, tile, block, first, count, each),
        grid_spec=pltpu.PrefetchScalarGridSpec(
            num_scalar_prefetch=1,
            grid=(turns,),
            in_specs=[cols(total), cols(keys), cols(keys), cols(total)]
            + [whole(l), whole(delta), whole(idr), whole(idk), rowspec(keys // turns, width)] + [apart] * len(after),
            out_specs=[rowspec(total // turns, columns), rowspec(keys // turns, columns), rowspec(keys // turns, columns), whole(grad)],
            scratch_shapes=[
                pltpu.VMEM((total, columns), bf16), pltpu.VMEM((total, LANES), jnp.int32), pltpu.VMEM((total, columns), f32),
                pltpu.VMEM((keys, columns), f32), pltpu.VMEM((keys, columns), f32), pltpu.VMEM((2, width, columns), f32),
            ],
        ),
        out_shape=[sds((total, columns), bf16), sds((keys, columns), bf16), sds((keys, columns), bf16), grad],
        name="cross_backward",
        **params(5 * count + 4, 10 * count + 4),
    )(items, *placed(q2, k2, v2, do, l, delta), idr, idk, *placed(memory), *after)


def memory_grad_kernel(ka_ref, kb_ref, va_ref, vb_ref, wk_ref, wv_ref, *rest):
    total = mm(jnp.concatenate([ka_ref[...], kb_ref[...]], axis=1), wk_ref[0], NT)
    total += mm(jnp.concatenate([va_ref[...], vb_ref[...]], axis=1), wv_ref[0], NT)
    rest[-1][...] = total.astype(bf16)


def memory_grad(ka, kb, va, vb, weights, index, after, rows=1024):
    keys, width = ka.shape[0], weights.shape[2]
    rowspec = lambda w: pl.BlockSpec((rows, w), lambda i: (i, 0))
    return pl.pallas_call(
        memory_grad_kernel,
        grid=(keys // rows,),
        in_specs=[rowspec(a.shape[1]) for a in (ka, kb, va, vb)] + [part(weights, index, width, 0), part(weights, index + 1, width, 0)] + [apart] * len(after),
        out_specs=rowspec(width),
        out_shape=out_array((keys, width), bf16),
        name="memory_grad",
        **params(4, 16),
    )(ka, kb, va, vb, weights, weights, *after)


def between_kernel(
    core_ref, ga_ref, gb_ref, gn23_ref, r1_ref, dr2_ref, dr3_ref, dqa_ref, dqb_ref, h1b_ref, o1_ref, wso_ref, wcq_ref, norms_ref, *rest
):
    dsum_ref, do1_ref, delta_ref, keep_ref, send_ref, gn_ref, total = rest[-7:]
    step = pl.program_id(0)

    @pl.when(step == 0)
    def _():
        total[...] = jnp.zeros_like(total)
        gn_ref[...] = jnp.zeros_like(gn_ref)

    dq2 = jnp.concatenate([dqa_ref[...], dqb_ref[...]], axis=1)
    dh1 = dr2_ref[...].astype(f32) + mm(dq2, wcq_ref[0], NT)
    n1, rstd1 = norm_rows(r1_ref[...].astype(f32))
    gn_ref[0:1, :] += column_sums(dh1 * n1)
    gn_ref[1:2, :] += column_sums(dh1)
    dr1 = norm_back(dh1, n1, rstd1, norms_ref[0:1, :])
    dsum_ref[...] = (dr1 + dr3_ref[...].astype(f32)).astype(bf16)
    da1 = dr1.astype(bf16)
    o1 = o1_ref[...]
    do1 = mm(da1, wso_ref[0], NT).astype(bf16)
    do1_ref[...] = do1
    delta_ref[...] = head_columns(do1, o1)
    total[0] += mm(h1b_ref[...], dq2, TN)
    total[1] += mm(o1, da1, TN)

    @pl.when(step == pl.num_programs(0) - 1)
    def _():
        gn_ref[2:6, :] = gn23_ref[...]
        r, width = keep_ref.shape[2:]
        norm_part = jnp.concatenate([gn_ref[...], jnp.zeros((r - 8, width), f32)]).astype(bf16)

        def write(device, ref, j):
            here = pl.ds(pl.multiple_of(device * r, r), r)
            for i in range(2):
                ref[j, i, :, : ga_ref.shape[2]] = ga_ref[i, here, :]
                ref[j, i, :, ga_ref.shape[2] :] = gb_ref[i, here, :]
                ref[j, 2 + i] = total[i, here, :].astype(bf16)
            ref[j, 4] = norm_part

        spread(keep_ref, send_ref, core_ref[0], write)


def between(core, pairs, ga, gb, gn23, r1, dr2, dr3, dqa, dqb, h1b, o1, weights, norms, after, rows=512):
    total, width = r1.shape
    rowspec = lambda w: pl.BlockSpec((rows, w), lambda i: (i, 0))
    sds = jax.ShapeDtypeStruct
    side = jax.ShapeDtypeStruct((pairs, 5, width // (2 * pairs), width), bf16)
    return pl.pallas_call(
        between_kernel,
        grid=(total // rows,),
        in_specs=[pl.BlockSpec(memory_space=pltpu.SMEM), whole(ga), whole(gb), whole(gn23)]
        + [rowspec(width)] * 3 + [rowspec(dqa.shape[1]), rowspec(dqb.shape[1])] + [rowspec(width)] * 2
        + [part(weights, 0, width, 0), part(weights, 1, width, 0), whole(norms)] + [apart] * len(after),
        out_specs=[rowspec(width)] * 2
        + [rowspec(LANES), whole(side), whole(side), pl.BlockSpec((8, width), lambda i: (0, 0))],
        out_shape=[sds((total, width), bf16), sds((total, width), bf16), sds((total, LANES), f32), side, side, sds((8, width), f32)],
        scratch_shapes=[pltpu.VMEM((2, width, width), f32)],
        name="between",
        **params(7, 24),
    )(core, ga, gb, gn23, *placed(r1), dr2, dr3, dqa, dqb, *placed(h1b, o1), weights, weights, norms, *after)


def self_backward_kernel(
    tile, block, core_ref, items_ref, q_ref, k_ref, v_ref, do_ref, l_ref, delta_ref, idr_ref, x_ref, wq_ref, wk_ref, wv_ref, sofar_ref, *rest
):
    gx_ref, keep_ref, send_ref, q_all, ids_all, dq, dk, dv, grads = rest[-9:]
    step = pl.program_id(0)
    total, width = q_ref.shape

    @pl.when(step == 0)
    def _():
        dq[...] = jnp.zeros_like(dq)
        dk[...] = jnp.zeros_like(dk)
        dv[...] = jnp.zeros_like(dv)
        grads[...] = jnp.zeros_like(grads)
        q_all[...] = q_ref[...] * jnp.asarray(HD ** -0.5, bf16)
        for j in range(total // block):
            ids_all[j * block : (j + 1) * block, :] = column_of(idr_ref[:, j * block : (j + 1) * block])
        attend_back(
            items_ref, idr_ref, ids_all, q_all, do_ref, k_ref, v_ref, l_ref, delta_ref, dq, dk, dv, tile, block, 0, True, 2
        )

    x = x_ref[...]
    rows = x.shape[0]
    here = pl.ds(pl.multiple_of(step * rows, rows), rows)
    gx = sofar_ref[...].astype(f32)
    parts = (dq[here, :] * HD ** -0.5).astype(bf16), dk[here, :].astype(bf16), dv[here, :].astype(bf16)
    for i, (grad, w_ref) in enumerate(zip(parts, (wq_ref, wk_ref, wv_ref))):
        gx += mm(grad, w_ref[0], NT)
        grads[i] += mm(x, grad, TN)
    gx_ref[...] = gx.astype(bf16)

    @pl.when(step == pl.num_programs(0) - 1)
    def _():
        r = keep_ref.shape[2]

        def write(device, ref, j):
            place = pl.ds(pl.multiple_of(device * r, r), r)
            for i in range(3):
                ref[j, i] = grads[i, place, :].astype(bf16)

        spread(keep_ref, send_ref, core_ref[0], write)


def self_backward(core, pairs, items, q, k, v, do, l, delta, idr, x, weights, sofar, after, turns=2, block=QROWS, tile=256):
    total, width = x.shape
    sds = jax.ShapeDtypeStruct
    side = sds((pairs, 3, width // (2 * pairs), width), bf16)
    rowspec = lambda w: pl.BlockSpec((total // turns, w), lambda i, *_: (i, 0))
    return pl.pallas_call(
        functools.partial(self_backward_kernel, tile, block),
        grid_spec=pltpu.PrefetchScalarGridSpec(
            num_scalar_prefetch=2,
            grid=(turns,),
            in_specs=[whole(a) for a in (q, k, v, do, l, delta, idr)]
            + [rowspec(width)] + [part(weights, i, width, 0) for i in range(3)] + [rowspec(width)] + [apart] * len(after),
            out_specs=[rowspec(width), whole(side), whole(side)],
            scratch_shapes=[
                pltpu.VMEM((total, width), bf16), pltpu.VMEM((total, LANES), jnp.int32),
                pltpu.VMEM((total, width), f32), pltpu.VMEM((total, width), f32), pltpu.VMEM((total, width), f32),
                pltpu.VMEM((3, width, width), f32),
            ],
        ),
        out_shape=[sds((total, width), bf16), side, side],
        name="self_backward",
        **params(17, 34),
    )(core, items, q, k, v, do, l, delta, idr, x, weights, weights, weights, sofar, *after)


def add_split_kernel(count, here_ref, *refs):
    places = refs[0].shape[1]
    for m in range(places):
        at = here_ref[0] ^ m
        total = refs[0][:, at].astype(f32)
        for ref in refs[1:count]:
            total += ref[:, at].astype(f32)
        refs[count + m][...] = total.astype(bf16)


def add_split(here, parts, outer, places):
    tail = parts[0].shape[1:]
    parts = [p.reshape((outer, places) + tail) for p in parts]
    out = pl.pallas_call(
        functools.partial(add_split_kernel, len(parts)),
        grid=(outer,),
        in_specs=[pl.BlockSpec(memory_space=pltpu.SMEM)] + [pl.BlockSpec((1, places) + tail, lambda i: (i, 0, 0, 0, 0))] * len(parts),
        out_specs=[pl.BlockSpec((1,) + tail, lambda i: (i, 0, 0, 0))] * places,
        out_shape=[jax.ShapeDtypeStruct((outer,) + tail, bf16)] * places,
        name="add_split",
        **params(3, 24),
    )(here, *parts)
    return list(out)


def first_pair_kernel(cut, here_ref, keep, came, *outs):
    for m in range(2):
        at = here_ref[0] ^ m
        outs[m][0] = (keep[0, :, at, :cut].astype(f32) + came[0, :, at, :cut].astype(f32)).astype(bf16)
        at = here_ref[1] ^ m
        outs[2 + m][0] = (keep[0, at, :, cut:].astype(f32) + came[0, at, :, cut:].astype(f32)).astype(bf16)


def first_pair(here, keep, came, outer, cut):
    squares, rows, width = keep.shape[1:]
    parts = [p.reshape(outer, 2, 2, squares, rows, width) for p in (keep, came)]
    shapes = [(outer, 2, n, rows, width) for n in (cut, cut, squares - cut, squares - cut)]
    out = pl.pallas_call(
        functools.partial(first_pair_kernel, cut),
        grid=(outer,),
        in_specs=[pl.BlockSpec(memory_space=pltpu.SMEM)] + [pl.BlockSpec((1,) + p.shape[1:], lambda i: (i, 0, 0, 0, 0, 0)) for p in parts],
        out_specs=[pl.BlockSpec((1,) + s[1:], lambda i: (i, 0, 0, 0, 0)) for s in shapes],
        out_shape=[jax.ShapeDtypeStruct(s, bf16) for s in shapes],
        name="first_pair",
        **params(2, 24),
    )(here, *parts)
    return list(out)


def second_pair_kernel(here_ref, keep_a, came_a, keep_b, came_b, *outs):
    for m in range(2):
        at = here_ref[1] ^ m
        outs[m][0] = (keep_a[0, at].astype(f32) + came_a[0, at].astype(f32)).astype(bf16)
        at = here_ref[0] ^ m
        outs[2 + m][0] = (keep_b[0, at].astype(f32) + came_b[0, at].astype(f32)).astype(bf16)


def second_pair(here, parts):
    outer = parts[0].shape[0]
    shapes = [(p.shape[0],) + p.shape[2:] for p in parts]
    out = pl.pallas_call(
        second_pair_kernel,
        grid=(outer,),
        in_specs=[pl.BlockSpec(memory_space=pltpu.SMEM)] + [pl.BlockSpec((1,) + p.shape[1:], lambda i: (i, 0, 0, 0, 0)) for p in parts],
        out_specs=[pl.BlockSpec((1,) + s[1:], lambda i: (i, 0, 0, 0)) for s in shapes],
        out_shape=[jax.ShapeDtypeStruct(s, bf16) for s in shapes],
        name="second_pair",
        **params(1, 24),
    )(here, *parts)
    return list(out)


def join_split_kernel(here_ref, keep_a, came_a, keep_b, came_b, *outs):
    cut = keep_a.shape[2]
    for m, out in enumerate(outs):
        at = here_ref[0] ^ m
        out[:, :cut] = (keep_a[:, at].astype(f32) + came_a[:, at].astype(f32)).astype(bf16)
        out[:, cut:] = (keep_b[:, at].astype(f32) + came_b[:, at].astype(f32)).astype(bf16)


def join_split(here, parts, outer, places):
    parts = [p.reshape((outer, places) + p.shape[1:]) for p in parts]
    tail = (parts[0].shape[2] + parts[2].shape[2],) + parts[0].shape[3:]
    out = pl.pallas_call(
        join_split_kernel,
        grid=(outer,),
        in_specs=[pl.BlockSpec(memory_space=pltpu.SMEM)] + [pl.BlockSpec((1,) + p.shape[1:], lambda i: (i, 0, 0, 0, 0)) for p in parts],
        out_specs=[pl.BlockSpec((1,) + tail, lambda i: (i, 0, 0, 0))] * places,
        out_shape=[jax.ShapeDtypeStruct((outer,) + tail, bf16)] * places,
        name="join_split",
        **params(1, 24),
    )(here, *parts)
    return list(out)


def place_kernel(here_ref, *refs):
    out_ref = refs[-1]
    for m, ref in enumerate(refs[:-1]):
        out_ref[0, :, here_ref[0] ^ m] = ref[0]


def place(here, pieces):
    shape = pieces[0].shape
    pieces = [p.reshape((shape[0], -1) + shape[-2:]) for p in pieces]
    count, tail = len(pieces), pieces[0].shape[2:]
    inner = pieces[0].shape[1]
    out = pl.pallas_call(
        place_kernel,
        grid=(shape[0],),
        in_specs=[pl.BlockSpec(memory_space=pltpu.SMEM)] + [pl.BlockSpec((1, inner) + tail, lambda i: (i, 0, 0, 0))] * count,
        out_specs=pl.BlockSpec((1, inner, count) + tail, lambda i: (i, 0, 0, 0, 0)),
        out_shape=jax.ShapeDtypeStruct((shape[0], inner, count) + tail, bf16),
        name="place",
        **params(1, 16),
    )(here, *pieces)
    return out.reshape(shape[:-2] + (count,) + tail)


def own_block(shape):
    return pl.BlockSpec(shape, lambda *_: (0,) * len(shape))


def pack_kernel(moves, count, *refs):
    ins, out_ref, wide = refs[:count], refs[count], refs[count + 1 :]
    rows = out_ref.shape[1]
    for ref, w in zip(ins, wide):
        w[...] = ref[...].astype(f32)
    for source, begin, step, square, block in moves:
        value = wide[source][pl.ds(begin, rows, stride=step), :]
        out_ref[square, :, block * LANES : (block + 1) * LANES] = value.astype(bf16)


def pack(arrays, moves, squares, rows, width, name):
    arrays = [a.reshape(-1, LANES) for a in arrays]
    return pl.pallas_call(
        functools.partial(pack_kernel, moves, len(arrays)),
        in_specs=[own_block(a.shape) for a in arrays],
        out_specs=own_block((squares, rows, width)),
        out_shape=jax.ShapeDtypeStruct((squares, rows, width), bf16),
        scratch_shapes=[pltpu.VMEM(a.shape, f32) for a in arrays],
        name=name,
        **params(1, 16),
    )(*placed(*arrays))


def square_moves(source, square, width):
    blocks = width // LANES
    return [(source, b, blocks, square, b) for b in range(blocks)]


def finish_kernel(moves, count, *refs):
    ins, outs = refs[:count], refs[count:]
    rows = ins[0].shape[1]
    for square, block, out, begin, step in moves:
        cols = slice(block * LANES, (block + 1) * LANES)
        total = ins[0][square, :, cols].astype(f32)
        for ref in ins[1:]:
            total += ref[square, :, cols].astype(f32)
        if step:
            outs[out][pl.ds(begin, rows, stride=step), :] = total
        else:
            outs[out][:, cols] = total


def finish(parts, moves, shapes, name):
    return pl.pallas_call(
        functools.partial(finish_kernel, moves, len(parts)),
        in_specs=[own_block(p.shape) for p in parts],
        out_specs=[own_block(s) for s in shapes],
        out_shape=[jax.ShapeDtypeStruct(s, f32) for s in shapes],
        name=name,
        **params(1, 16),
    )(*parts)


def fill_items(ref, first, high, keys, block, tile):
    filled = jnp.int32(0)
    for b in range(len(first)):
        count = (high[b] - first[b] * LANES + tile - 1) // tile

        def put(j, at, b=b):
            ref[0, at] = b
            ref[1, at] = first[b] + j * (tile // LANES)
            return at + 1

        filled = lax.fori_loop(0, count, put, filled)
    for j in range(PADDING):
        ref[0, filled + j] = len(first) - 1
        ref[1, filled + j] = keys // LANES
    for i, n in enumerate(EACH):
        ref[2, i] = (filled + n - 1) // n


def plan_kernel(block, tile, seg_ref, mem_ref, qid_ref, mid_ref, own_ref, cross_ref):
    def ends_of(ref):
        ends, total = [], jnp.int32(0)
        for i in range(ref.shape[1]):
            total += ref[0, i]
            ends.append(total)
        return ends

    ends, mem_ends = ends_of(seg_ref), ends_of(mem_ref)
    for ref, marks in ((qid_ref, ends), (mid_ref, mem_ends)):
        places = lax.broadcasted_iota(jnp.int32, ref.shape, 1)
        ids = jnp.zeros(ref.shape, jnp.int32)
        for mark in marks:
            ids += (places >= mark).astype(jnp.int32)
        ref[...] = ids
    total, keys = qid_ref.shape[1], mid_ref.shape[1]
    own, low, high = [], [], []
    for begin in range(0, total, block):
        own_first, first, last = jnp.int32(0), jnp.int32(0), mem_ref[0, 0]
        for i in range(seg_ref.shape[1]):
            passed = (ends[i] <= begin).astype(jnp.int32)
            own_first += passed * seg_ref[0, i]
            first += passed * mem_ref[0, i]
            if i + 1 < seg_ref.shape[1]:
                last += (ends[i] <= begin + block - 1).astype(jnp.int32) * mem_ref[0, i + 1]
        own.append(own_first // LANES)
        low.append(first // LANES)
        high.append(last)
    fill_items(own_ref, own, [begin + block for begin in range(0, total, block)], total, block, tile)
    fill_items(cross_ref, low, high, keys, block, tile)


def plan(seg, mem, total, keys, block=QROWS, tile=256):
    smem = pl.BlockSpec(memory_space=pltpu.SMEM)
    sds = jax.ShapeDtypeStruct
    more = PADDING
    return pl.pallas_call(
        functools.partial(plan_kernel, block, tile),
        in_specs=[smem, smem],
        out_specs=[own_block((1, total)), own_block((1, keys)), smem, smem],
        out_shape=[
            sds((1, total), jnp.int32), sds((1, keys), jnp.int32),
            sds((3, total // block * (total // tile) + more), jnp.int32), sds((3, total // block * (keys // tile) + more), jnp.int32),
        ],
        name="plan",
        **params(1, 16),
    )(seg, mem)

HEAD_START = 1


def mesh_size():
    return lax.axis_size("dp") * lax.axis_size("fsdp")


def position():
    return lax.axis_index("dp") * lax.axis_size("fsdp") + lax.axis_index("fsdp")


def bit_groups(wide):
    count = mesh_size().bit_length() - 1
    groups = [(0, 1)]
    while groups[-1][0] + groups[-1][1] < count:
        low = groups[-1][0] + groups[-1][1]
        groups.append((low, min(2 if len(groups) <= wide else 1, count - low)))
    return groups


def swap(x, mask):
    return lax.ppermute(x, ("dp", "fsdp"), [(i, i ^ mask) for i in range(mesh_size())])


def place_in(group):
    return (position() >> group[0]) & ((1 << group[1]) - 1)


def tie(x, *after):
    return lax.optimization_barrier((x, *after))[0] if after else x


def gather_step(x, group, after=(), lower=0, came=None):
    low, width = group
    here = place_in(group)
    if came is None:
        came = tie([swap(x, m << low) for m in range(1, 1 << width)], *after)
    blocks = [x] + came
    for j in range(width):
        flip = (here >> j) & 1 == 1
        blocks = [jnp.where(flip, blocks[p ^ (1 << j)], blocks[p]) for p in range(1 << width)]
    return jnp.stack(blocks, axis=x.ndim - 2 - lower)


def gathered(x):
    return x.reshape(x.shape[:1] + (-1, x.shape[-1]))


def swap_pieces(parts, group, after=()):
    return [parts[0]] + tie([swap(parts[m], m << group[0]) for m in range(1, len(parts))], *after)


def next_pieces(parts, groups, done):
    group = groups[done]
    outer = 1 << sum(g[1] for g in groups[done + 1 :])
    return add_split(place_in(group).reshape(1).astype(jnp.int32), parts, outer, 1 << group[1])


def norm_parts(norm_params, size):
    parts, left = [], norm_params
    for _ in range(3):
        part = left.astype(bf16)
        parts.append(jnp.pad(part, (0, LANES - part.size)))
        left = left - part.astype(f32)
    flat = jnp.concatenate(parts)
    return jnp.pad(flat, (0, size - flat.size))


def resplit(keep, send, devices, core, squares):
    halves = jnp.concatenate([keep, send])
    width = halves.shape[-1]
    first = halves[:, :squares].transpose(1, 0, 2, 3).reshape(squares, devices, -1, width).transpose(1, 0, 2, 3)
    rows = first.shape[2]
    if halves.shape[1] > squares:
        rest = halves[:, squares:].reshape(devices, halves.shape[1] - squares, rows, width)
        first = jnp.concatenate([first, rest], axis=1)
    both = first.reshape(devices // 2, 2, -1, rows, width)
    return [lax.dynamic_index_in_dim(both, core ^ m, 1, keepdims=False) for m in range(2)]


def body(
    inputs, memory, seg_lengths, mem_lengths, self_query, self_key, self_value, self_out,
    cross_query, cross_key, cross_value, cross_out, ffn_in, ffn_out, norm_params, cotangent,
):
    total, width = inputs.shape
    keys = memory.shape[0]
    devices = mesh_size()
    groups, single = bit_groups(8), bit_groups(1)
    down = groups[::-1]
    shard = norm_params.shape[0]
    size = self_query.shape[0]
    own_rows = size // width
    blocks = ffn_in.shape[0] // size
    whole_tiles = own_rows % 16 == 0
    core = place_in(groups[0]).reshape(1).astype(jnp.int32)

    firsts = (self_query, self_key, self_value)
    seconds = (self_out, cross_query, cross_key, cross_value, norm_parts(norm_params, size))
    if whole_tiles:
        lane_blocks = width // LANES
        three = [m for i in range(3) for m in square_moves(i, i, width)]
        five = three + [m for i in range(3, 5) for m in square_moves(i, i, width)]
        wide = [(0, c * lane_blocks + b, blocks * lane_blocks, c, b) for c in range(blocks) for b in range(lane_blocks)]
        tall = [(1, j * own_rows * lane_blocks + b, lane_blocks, blocks + 1 + j, b) for j in range(blocks) for b in range(lane_blocks)]
        first = pack(firsts, three, 3, own_rows, width, "pack_self")
        second = pack(tie(seconds, first), five, 5, own_rows, width, "pack_cross")
        last = square_moves(2, blocks, width)
        third = pack(tie((ffn_in, ffn_out, cross_out), first), wide + tall + last, 2 * blocks + 1, own_rows, width, "pack_ffn")
    else:
        first = jnp.concatenate(firsts).reshape(3, own_rows, width)
        second = jnp.concatenate(seconds).reshape(5, own_rows, width)
        fi = ffn_in.reshape(own_rows, blocks, width).transpose(1, 0, 2)
        third = jnp.concatenate([fi, cross_out.reshape(1, own_rows, width), ffn_out.reshape(blocks, own_rows, width)])
    third = third.reshape(-1, width)
    plane = groups[1]
    high_bits = [(b, 1) for b in reversed(range(plane[0] + plane[1], devices.bit_length() - 1))]
    for g in down[:-2]:
        first = gather_step(first, g)
    second = gather_step(second, high_bits[0])
    qid, mid, own_items, items = plan(*tie((seg_lengths, mem_lengths), first), total, keys)
    first = gather_step(first, plane, [second, own_items])
    for g in high_bits[1:]:
        second = gather_step(second, g)
    third = gather_step(third, high_bits[0])
    first = gathered(gather_step(first, down[-1], [second, third]))
    for g in high_bits[1:]:
        third = gather_step(third, g)
    low, high = (plane[0], 1), (plane[0] + 1, 1)
    cut = (blocks + 1) * own_rows
    part_a, part_b = tie((third[..., :cut, :], third[..., cut:, :]), first)
    early = [second, part_a, part_b]
    bits = jnp.stack([(position() >> b) & 1 for b in (low[0], high[0], 0)]).astype(jnp.int32)
    pairs = devices // 2 if whole_tiles else 1
    part_of = core if whole_tiles else jnp.zeros_like(core)

    q1, k1, v1, o1, l1 = self_forward(own_items, inputs, first, qid, early)
    def at(group):
        return place_in(group).reshape(1).astype(jnp.int32)

    second = gather_step(second, plane, [l1])
    came_a, came_b = tie((swap(part_a, 1 << low[0]), swap(part_b, 1 << high[0])), l1)
    second = tie(second, came_a, came_b)
    part_a, part_b = place(at(low), [part_a, came_a]), place(at(high), [part_b, came_b])
    second = gathered(gather_step(second, down[-1]))
    norm_all = second[4].reshape(devices, -1)[:, : 3 * LANES].reshape(devices, 3, LANES)[:, :, :shard].astype(f32)
    norms = jnp.sum(norm_all, axis=1).reshape(6, width)
    k2, v2, r1, h1b, q2, h1, o2, l2 = cross_forward(items, memory, inputs, o1, second, norms, qid, mid, [bits])
    part_a, part_b = [part_a, swap(part_a, 1 << high[0])], [part_b, swap(part_b, 1 << low[0])]
    came = [swap(part_a[0], 1), swap(part_b[0], 1)]
    part_a[1], part_b[1], came[0], came[1] = tie((part_a[1], part_b[1], came[0], came[1]), l2)
    part_a += [came[0], swap(part_a[1], 1)]
    part_b += [came[1], swap(part_b[1], 1)]
    if whole_tiles:
        pieces = [p.reshape((-1, 2) + p.shape[-2:]) for p in part_a + part_b]
    else:
        pieces = []
        for parts, group, lower in ((part_a, high, 1), (part_b, low, 0)):
            halves = [gather_step(parts[j], group, lower=lower, came=[parts[j + 1]]) for j in (0, 2)]
            both = gather_step(halves[0], down[-1], came=[halves[1]]).reshape(devices, -1, own_rows, width)
            pieces.append(both)
        pieces[0] = jnp.concatenate([pieces[0][:, i].reshape(width, width) for i in range(blocks + 1)])[None]
        pieces[1] = pieces[1].reshape(1, -1, width)
    out, dr3, dr2, do2, delta2, keep, send, gn23 = ffn(part_of, bits, pairs, h1, inputs, cotangent, o2, pieces, norms)

    one = [keep, send] if whole_tiles else resplit(keep, send, devices, core[0], blocks + 1)
    dq2a, dk2a, dv2a, gckva = cross_backward(items, q2, k2, v2, do2, l2, delta2, qid, mid, memory, 0, HEAD_START, 4, [])
    low, high = 1 << groups[1][0], 2 << groups[1][0]
    both = jnp.stack([(position() >> (groups[1][0] + j)) & 1 for j in range(2)]).astype(jnp.int32)
    one = swap_pieces(one, groups[0], [dq2a])
    one = first_pair(both, one[0], one[1], devices // 8, blocks + 1)
    more = width // LANES - HEAD_START
    dq2b, dk2b, dv2b, gckvb = cross_backward(
        items, q2, k2, v2, do2, l2, delta2, qid, mid, memory, HEAD_START, more, 2, [one[1], one[3]]
    )
    came = tie([swap(one[1], low), swap(one[3], high)], dq2b)
    one = second_pair(both, [one[0], came[0], one[2], came[1]])
    gm = memory_grad(dk2a, dk2b, dv2a, dv2b, second, 2, [one[1], one[3]])
    dsum, do1, delta1, keep, send, gn = between(
        part_of, pairs, gckva, gckvb, gn23, r1, dr2, dr3, dq2a, dq2b, h1b, o1, second, norms, placed(gm)
    )
    came = tie([swap(one[1], high), swap(one[3], low)], do1)
    one = join_split(
        place_in(single[2]).reshape(1).astype(jnp.int32), [one[0], came[0], one[2], came[1]],
        1 << sum(g[1] for g in single[3:]), 1 << single[2][1],
    )
    two = [keep, send]
    if not whole_tiles:
        two = resplit(keep, send, devices, core[0], 5)
        own_norms = jnp.pad(gn[:6].astype(bf16).reshape(devices, -1), ((0, 0), (0, size - shard)))
        own_norms = own_norms.reshape(devices // 2, 2, own_rows, width)
        two = [two[m].at[:, 4].set(lax.dynamic_index_in_dim(own_norms, core[0] ^ m, 1, keepdims=False)) for m in range(2)]
    two = next_pieces(swap_pieces(tie(two, one[1]), groups[0]), groups, 1)
    gx, keep, send = self_backward(part_of, pairs, own_items, q1, k1, v1, do1, l1, delta1, qid, inputs, first, dsum, one[1:] + two[1:])
    two = next_pieces(swap_pieces(two, groups[1], [gx]), single, 2)
    one = next_pieces(swap_pieces(one, single[2], [gx]), single, 3)
    keep, send = tie((keep, send), two[1], one[1])
    three = [keep, send] if whole_tiles else resplit(keep, send, devices, core[0], 3)
    three = next_pieces(swap_pieces(three, groups[0]), groups, 1)
    for i in range(2, len(groups)):
        three = next_pieces(swap_pieces(three, groups[i - 1]), groups, i)
    for i in range(3, len(single)):
        two = next_pieces(swap_pieces(two, single[i - 1]), single, i)
        if i > 3:
            one = next_pieces(swap_pieces(one, single[i - 1]), single, i)

    def flat(g):
        return g.reshape(-1)

    chains = [swap_pieces(one, single[-1], [three[1]]), swap_pieces(two, single[-1], [three[1]]), swap_pieces(three, groups[-1])]
    chains = [[p.reshape(-1, own_rows, width) for p in chain] for chain in chains]
    if whole_tiles:
        lane_rows = size // LANES
        square, long = (lane_rows, LANES), (blocks * lane_rows, LANES)

        moves = [(c, b, 0, c * lane_blocks + b, blocks * lane_blocks) for c in range(blocks) for b in range(lane_blocks)]
        moves += [(blocks, b, 1, b, lane_blocks) for b in range(lane_blocks)]
        moves += [
            (blocks + 1 + j, b, 2, j * own_rows * lane_blocks + b, lane_blocks) for j in range(blocks) for b in range(lane_blocks)
        ]
        gfi, gco, gfo = finish(chains[0], moves, [long, square, long], "finish_ffn")
        moves = [(i, b, i, b, lane_blocks) for i in range(4) for b in range(lane_blocks)] + [(4, b, 4, 0, 0) for b in range(lane_blocks)]
        gck, gcv, gcq, gso, gn = finish(chains[1], moves, [square] * 4 + [(own_rows, width)], "finish_cross")
        gn = lax.dynamic_slice_in_dim(flat(gn[:6]), position() * shard, shard)
        moves = [(i, b, i, b, lane_blocks) for i in range(3) for b in range(lane_blocks)]
        gsq, gsk, gsv = finish(chains[2], moves, [square] * 3, "finish_self")
    else:
        one, two, three = (sum(p.astype(f32) for p in chain) for chain in chains)
        gfi, gco, gfo = one[:blocks].transpose(1, 0, 2), one[blocks], one[blocks + 1 :]
        gck, gcv, gcq, gso, gn = two[0], two[1], two[2], two[3], flat(two[4])[:shard]
        gsq, gsk, gsv = three[0], three[1], three[2]
    return (out, gx, gm) + tuple(flat(g) for g in (gsq, gsk, gsv, gso, gcq, gck, gcv, gco, gfi, gfo, gn))


def solution(mesh):
    rows, flat = P(("dp", "fsdp"), None), P(("dp", "fsdp"))
    return jax.shard_map(
        body,
        mesh=mesh,
        in_specs=(rows,) * 4 + (flat,) * 11 + (rows,),
        out_specs=(rows,) * 3 + (flat,) * 11,
        check_vma=False,
    )
```

profile of v0, /device:TPU:0, one launch (start us, length us, event | category | flops | bytes accessed | tf_op | source)
XLA Modules:
  0.0 203.5 jit_solution(3789197541405377040)
XLA Ops:
  1.4 3.1 %collective-permute-start.2 = (bf16[3,16,512]{2,1,0:T(8,128)(2,1)S(1)}, bf16[3,16,512]{2,1,0:T(8,128)(2,1)S(1)}, u32[]{:S(2)}, u32[]{:S(2)}) collective-permute-start(bf16[3,16,512]{2,1,0:T(8,128)(2,1)S(1)} %pack_self.1), channel_id=1, source_target_pairs={{0,8},{1,9},{2,10},{3,11},{4,12},{5,13},{6,14},{7,15},{8,0},{9,1},... | collective-permute-start | bytes 147464 | tf_op jit(solution)/shard_map/ppermute | solution.py:989
  4.5 2.6 %collective-permute-start.1 = (bf16[3,16,512]{2,1,0:T(8,128)(2,1)S(1)}, bf16[3,16,512]{2,1,0:T(8,128)(2,1)S(1)}, u32[]{:S(2)}, u32[]{:S(2)}) collective-permute-start(bf16[3,16,512]{2,1,0:T(8,128)(2,1)S(1)} %pack_self.1), channel_id=1, source_target_pairs={{0,16},{1,17},{2,18},{3,19},{4,20},{5,21},{6,22},{7,23},{8,24},{9,... | collective-permute-start | bytes 147464 | tf_op jit(solution)/shard_map/ppermute | solution.py:989
  7.8 0.8 pack_cross.1
  8.6 2.0 collective-permute-start.3
  10.5 1.0 pack_ffn.1
  11.5 1.1 collective-permute-start.12
  12.6 1.0 collective-permute-done
  13.7 2.5 %collective-permute-start.10 = (bf16[3,4,16,512]{3,2,0,1:T(8,128)(2,1)S(1)}, bf16[3,4,16,512]{3,2,0,1:T(8,128)(2,1)S(1)}, u32[]{:S(2)}, u32[]{:S(2)}) collective-permute-start(bf16[3,4,16,512]{3,2,0,1:T(8,128)(2,1)S(1)} %pad_maximum_fusion.7), channel_id=1, source_target_pairs={{0,6},{1,7},{2,4},{3,5},{4,2},{5,3},{6,0},{7,1},{8,14},{9,15},{10,... | collective-permute-start | bytes 589832 | tf_op jit(solution)/shard_map/ppermute | solution.py:989
  17.2 2.2 %plan.1 = (s32[1,1024]{1,0:T(1,128)S(1)}, s32[1,2048]{1,0:T(1,128)S(1)}, s32[3,36]{1,0:T(4,128)S(1)}, s32[3,68]{1,0:T(4,128)S(1)}) custom-call(s32[1,16]{1,0:T(1,128)S(1)} %copy-done.7, s32[1,17]{1,0:T(1,128)S(1)} %copy-done.8), custom_call_target="tpu_custom_call" | custom-call | flops 1000000000 | bytes 1048576 | tf_op jit(solution)/shard_map/plan/pallas_call | solution.py:956
  20.1 2.0 collective-permute-done.12
  22.2 1.1 collective-permute-done.9
  23.8 2.6 %collective-permute-done.4 = bf16[5,2,16,512]{3,2,1,0:T(8,128)(2,1)S(1)} collective-permute-done((bf16[5,2,16,512]{3,2,1,0:T(8,128)(2,1)S(1)}, bf16[5,2,16,512]{3,2,1,0:T(8,128)(2,1)S(1)}, u32[]{:S(2)}, u32[]{:S(2)}) %collective-permute-start.4) | collective-permute-done | bytes 163872 | tf_op jit(solution)/shard_map/ppermute | solution.py:989
  26.5 2.5 %collective-permute-start.7 = (bf16[5,2,2,16,512]{4,3,2,1,0:T(8,128)(2,1)S(1)}, bf16[5,2,2,16,512]{4,3,2,1,0:T(8,128)(2,1)S(1)}, u32[]{:S(2)}, u32[]{:S(2)}) collective-permute-start(bf16[5,2,2,16,512]{4,3,2,1,0:T(8,128)(2,1)S(1)} %pad_maximum_fusion.4.rest_0_), channel_id=1, source_target_pairs={{0,6},{1,7},{2,4},{3,5},{4,2},{5,3},{6,0},{7,1},{8,14},{9,15},{10,... | collective-permute-start | bytes 983048 | tf_op jit(solution)/shard_map/ppermute | solution.py:989
  30.0 1.5 collective-permute-done.13
  32.1 1.6 collective-permute-start.15
  33.7 1.5 collective-permute-start.14
  35.2 12.1 %self_forward.1 = (bf16[1024,512]{1,0:T(8,128)(2,1)}, bf16[1024,512]{1,0:T(8,128)(2,1)}, bf16[1024,512]{1,0:T(8,128)(2,1)}, bf16[1024,512]{1,0:T(8,128)(2,1)}, f32[1024,128]{1,0:T(8,128)}) custom-call(s32[3,36]{1,0:T(4,128)S(1)} %get-tuple-element.143.items_ref, bf16[1024,512]{1,0:T(8,128)(2,1)} %x_ref.7, bf16[3,512,512]{2,1,0:T(8,128)(2,1)S(1)} %bitcast.136, ...), custom_call_target="tpu_custom_call" | custom-call | flops 12999999488 | bytes 1048576 | tf_op jit(solution)/shard_map/self_forward/pallas_call | solution.py:247
  47.6 1.4 collective-permute-done.14.refs_1_
  49.1 0.8 place.3
  51.4 1.4 collective-permute-start.17
  52.8 1.5 select_bitcast_fusion.1
  55.4 18.5 %cross_forward.1 = (bf16[2048,512]{1,0:T(8,128)(2,1)}, bf16[2048,512]{1,0:T(8,128)(2,1)}, bf16[1024,512]{1,0:T(8,128)(2,1)}, bf16[1024,512]{1,0:T(8,128)(2,1)}, ...) custom-call(s32[3,68]{1,0:T(4,128)S(1)} %get-tuple-element.137.items_ref, ...), custom_call_target="tpu_custom_call" | custom-call | flops 19000000512 | bytes 1048576 | tf_op jit(solution)/shard_map/cross_forward/pallas_call | solution.py:321
  74.0 1.3 collective-permute-start.21
  75.3 2.6 %collective-permute-done.22 = bf16[2,2,2,64,512]{4,3,2,1,0:T(8,128)(2,1)S(1)} collective-permute-done((bf16[2,2,2,64,512]{4,3,2,1,0:T(8,128)(2,1)}, bf16[2,2,2,64,512]{4,3,2,1,0:T(8,128)(2,1)S(1)}, u32[]{:S(2)}, u32[]{:S(2)}) %collective-permute-start.22) | collective-permute-done | bytes 524320 | tf_op jit(solution)/shard_map/ppermute | solution.py:989
  79.0 29.1 %ffn.1 = (bf16[1024,512]{1,0:T(8,128)(2,1)}, bf16[1024,512]{1,0:T(8,128)(2,1)}, bf16[1024,512]{1,0:T(8,128)(2,1)}, bf16[1024,512]{1,0:T(8,128)(2,1)}, f32[1024,1...) custom-call(s32[1]{0:T(128)} %bitcast.core_ref, ...), custom_call_target="tpu_custom_call" | custom-call | flops 32000000000 | bytes 1048576 | tf_op jit(solution)/shard_map/ffn/pallas_call | solution.py:495
  108.6 8.9 %cross_backward.2 = (bf16[1024,128]{1,0:T(8,128)(2,1)S(1)}, bf16[2048,128]{1,0:T(8,128)(2,1)S(1)}, bf16[2048,128]{1,0:T(8,128)(2,1)S(1)}, bf16[2,512,128]{2,1,0:T(8,128)(2,1)S(1)}) custom-call(s32[3,68]{1,0:T(4,128)S(1)} %get-tuple-element.137.items_ref, bf16[1024,512]{1,0:T(8,128)(2,1)} %get-tuple-element.174.q2_ref, ...), custom_call_target="tpu_custom_call" | custom-call | flops 8999999488 | bytes 1048576 | tf_op jit(solution)/shard_map/cross_backward/pallas_call | solution.py:558
  117.6 1.2 first_pair.1
  119.8 18.5 %cross_backward.3 = (bf16[1024,384]{1,0:T(8,128)(2,1)S(1)}, bf16[2048,384]{1,0:T(8,128)(2,1)S(1)}, bf16[2048,384]{1,0:T(8,128)(2,1)S(1)}, bf16[2,512,384]{2,1,0:T(8,128)(2,1)S(1)}) custom-call(s32[3,68]{1,0:T(4,128)S(1)} %get-tuple-element.137.items_ref, bf16[1024,512]{1,0:T(8,128)(2,1)} %get-tuple-element.174.q2_ref, ...), custom_call_target="tpu_custom_call" | custom-call | flops 19000000512 | bytes 1048576 | tf_op jit(solution)/shard_map/cross_backward/pallas_call | solution.py:558
  138.3 0.9 second_pair.1
  139.2 1.9 collective-permute-start.27
  141.1 1.4 collective-permute-start.26
  142.5 3.6 %memory_grad.1.rest_0_ = bf16[2048,512]{1,0:T(8,128)(2,1)} custom-call(bf16[2048,128]{1,0:T(8,128)(2,1)S(1)} %get-tuple-element.193.ka_ref, bf16[2048,384]{1,0:T(8,128)(2,1)S(1)} %get-tuple-element.194.kb_ref, bf16[2048,128]{1,0:T(8,128)(2,1)S(1)} %get-tuple-element.195.va_ref, bf16[2048,384]{1,0:T(8,128)(2,1)S(1)} %get-tuple-element.196.vb_ref, ...), custom_call_target="tpu_custom_call" | custom-call | flops 4000000000 | bytes 1048576 | tf_op jit(solution)/shard_map/memory_grad/pallas_call | solution.py:586
  146.1 6.7 %between.1 = (bf16[1024,512]{1,0:T(8,128)(2,1)S(1)}, bf16[1024,512]{1,0:T(8,128)(2,1)S(1)}, f32[1024,128]{1,0:T(8,128)S(1)}, bf16[16,5,16,512]{3,2,1,0:T(8,128)(...) custom-call(s32[1]{0:T(128)} %bitcast.core_ref, bf16[2,512,128]{2,1,0:T(8,128)(2,1)S(1)} %get-tuple-element.179.ga_ref, ...), custom_call_target="tpu_custom_call" | custom-call | flops 7000000000 | bytes 1048576 | tf_op jit(solution)/shard_map/between/pallas_call | solution.py:645
  153.4 4.1 %collective-permute-start.32 = (bf16[2,9,16,512]{3,2,1,0:T(8,128)(2,1)S(1)}, bf16[2,9,16,512]{3,2,1,0:T(8,128)(2,1)S(1)}, u32[]{:S(2)}, u32[]{:S(2)}) collective-permute-start(bf16[2,9,16,512]{3,2,1,0:T(8,128)(2,1)S(1)} %get-tuple-element.210.rest_0_), channel_id=1, source_target_pairs={{0,8},{1,9},{2,10},{3,11},{4,12},{5,13},{6,14},{7,15},{8,0},{9,1},... | collective-permute-start | bytes 884744 | tf_op jit(solution)/shard_map/ppermute | solution.py:989
  158.5 1.9 collective-permute-start.30
  160.5 1.0 collective-permute-start.31
  161.5 15.4 %self_backward.1 = (bf16[1024,512]{1,0:T(8,128)(2,1)}, bf16[16,3,16,512]{3,2,1,0:T(8,128)(2,1)S(1)}, bf16[16,3,16,512]{3,2,1,0:T(8,128)(2,1)S(1)}) custom-call(s32[1]{0:T(128)} %bitcast.core_ref, s32[3,36]{1,0:T(4,128)S(1)} %get-tuple-element.143.items_ref, bf16[1024,512]{1,0:T(8,128)(2,1)S(1)} %copy-done.12, bf16[1024,512]{1,0:T(8,128)(2,1)S(1)} %copy-done.13, ...), custom_call_target="tpu_custom_call" | custom-call | flops 16999999488 | bytes 1048576 | tf_op jit(solution)/shard_map/self_backward/pallas_call | solution.py:707
  177.3 2.5 %collective-permute-start.42 = (bf16[1,9,16,512]{3,2,1,0:T(8,128)(2,1)S(1)}, bf16[1,9,16,512]{3,2,1,0:T(8,128)(2,1)S(1)}, u32[]{:S(2)}, u32[]{:S(2)}) collective-permute-start(bf16[1,9,16,512]{3,2,1,0:T(8,128)(2,1)S(1)} %get-tuple-element.228), channel_id=1, source_target_pairs={{0,16},{1,17},{2,18},{3,19},{4,20},{5,21},{6,22},{7,23},{8,24},{9,... | collective-permute-start | bytes 442376 | tf_op jit(solution)/shard_map/ppermute | solution.py:989
  180.4 0.9 collective-permute-start.34
  181.3 1.9 collective-permute-start.35
  183.9 4.1 %collective-permute-done.40 = bf16[2,5,16,512]{3,2,1,0:T(8,128)(2,1)S(1)} collective-permute-done((bf16[2,5,16,512]{3,2,1,0:T(8,128)(2,1)S(1)}, bf16[2,5,16,512]{3,2,1,0:T(8,128)(2,1)S(1)}, u32[]{:S(2)}, u32[]{:S(2)}) %collective-permute-start.40) | collective-permute-done | bytes 163872 | tf_op jit(solution)/shard_map/ppermute | solution.py:989
  188.1 2.8 %collective-permute-start.41 = (bf16[1,5,16,512]{3,2,1,0:T(8,128)(2,1)S(1)}, bf16[1,5,16,512]{3,2,1,0:T(8,128)(2,1)S(1)}, u32[]{:S(2)}, u32[]{:S(2)}) collective-permute-start(bf16[1,5,16,512]{3,2,1,0:T(8,128)(2,1)S(1)} %get-tuple-element.244), channel_id=1, source_target_pairs={{0,16},{1,17},{2,18},{3,19},{4,20},{5,21},{6,22},{7,23},{8,24},{9,... | collective-permute-start | bytes 245768 | tf_op jit(solution)/shard_map/ppermute | solution.py:989
  190.8 1.5 collective-permute-done.35
  192.5 2.2 %collective-permute-start.37 = (bf16[1,3,16,512]{3,2,1,0:T(8,128)(2,1)S(1)}, bf16[1,3,16,512]{3,2,1,0:T(8,128)(2,1)S(1)}, u32[]{:S(2)}, u32[]{:S(2)}) collective-permute-start(bf16[1,3,16,512]{3,2,1,0:T(8,128)(2,1)S(1)} %get-tuple-element.236), channel_id=1, source_target_pairs={{0,8},{1,9},{2,10},{3,11},{4,12},{5,13},{6,14},{7,15},{8,0},{9,1},... | collective-permute-start | bytes 147464 | tf_op jit(solution)/shard_map/ppermute | solution.py:989
  195.9 1.0 collective-permute-start.38
  196.9 1.5 collective-permute-start.39
  199.7 1.7 collective-permute-done.38
  201.4 1.5 collective-permute-done.39
  (141 shorter events, 17.5 us)
Async XLA Ops:
  1.4 11.2 %collective-permute-start.2 = (bf16[3,16,512]{2,1,0:T(8,128)(2,1)S(1)}, bf16[3,16,512]{2,1,0:T(8,128)(2,1)S(1)}, u32[]{:S(2)}, u32[]{:S(2)}) collective-permute-start(bf16[3,16,512]{2,1,0:T(8,128)(2,1)S(1)} %pack_self.1), channel_id=1, source_target_pairs={{0,8},{1,9},{2,10},{3,11},{4,12},{5,13},{6,14},{7,15},{8,0},{9,1},... | collective-permute-start | bytes 147464 | tf_op jit(solution)/shard_map/ppermute | solution.py:989
  4.5 8.1 %collective-permute-start.1 = (bf16[3,16,512]{2,1,0:T(8,128)(2,1)S(1)}, bf16[3,16,512]{2,1,0:T(8,128)(2,1)S(1)}, u32[]{:S(2)}, u32[]{:S(2)}) collective-permute-start(bf16[3,16,512]{2,1,0:T(8,128)(2,1)S(1)} %pack_self.1), channel_id=1, source_target_pairs={{0,16},{1,17},{2,18},{3,19},{4,20},{5,21},{6,22},{7,23},{8,24},{9,... | collective-permute-start | bytes 147464 | tf_op jit(solution)/shard_map/ppermute | solution.py:989
  7.1 6.5 %collective-permute-start = (bf16[3,16,512]{2,1,0:T(8,128)(2,1)S(1)}, bf16[3,16,512]{2,1,0:T(8,128)(2,1)S(1)}, u32[]{:S(2)}, u32[]{:S(2)}) collective-permute-start(bf16[3,16,512]{2,1,0:T(8,128)(2,1)S(1)} %pack_self.1), channel_id=1, source_target_pairs={{0,24},{1,25},{2,26},{3,27},{4,28},{5,29},{6,30},{7,31},{8,16},{9,... | collective-permute-start | bytes 147464 | tf_op jit(solution)/shard_map/ppermute | solution.py:989
  8.6 11.2 %collective-permute-start.3 = (bf16[5,16,512]{2,1,0:T(8,128)(2,1)S(1)}, bf16[5,16,512]{2,1,0:T(8,128)(2,1)S(1)}, u32[]{:S(2)}, u32[]{:S(2)}) collective-permute-start(bf16[5,16,512]{2,1,0:T(8,128)(2,1)S(1)} %pack_cross.1), channel_id=1, source_target_pairs={{0,16},{1,17},{2,18},{3,19},{4,20},{5,21},{6,22},{7,23},{8,24},{9,... | collective-permute-start | bytes 245768 | tf_op jit(solution)/shard_map/ppermute | solution.py:989
  10.5 6.7 %copy-start.7 = (s32[1,16]{1,0:T(1,128)S(1)}, s32[1,16]{1,0:T(1,128)}, u32[]{:S(2)}) copy-start(s32[1,16]{1,0:T(1,128)} %seg_ref) | copy-start | bytes 196
  10.5 6.7 %copy-start.8 = (s32[1,17]{1,0:T(1,128)S(1)}, s32[1,17]{1,0:T(1,128)}, u32[]{:S(2)}) copy-start(s32[1,17]{1,0:T(1,128)} %mem_ref) | copy-start | bytes 208
  11.5 10.6 %collective-permute-start.12 = (bf16[144,512]{1,0:T(8,128)(2,1)S(1)}, bf16[144,512]{1,0:T(8,128)(2,1)S(1)}, u32[]{:S(2)}, u32[]{:S(2)}) collective-permute-start(bf16[144,512]{1,0:T(8,128)(2,1)S(1)} %bitcast.142), channel_id=1, source_target_pairs={{0,16},{1,17},{2,18},{3,19},{4,20},{5,21},{6,22},{7,23},{8,24},{9,... | collective-permute-start | bytes 442376 | tf_op jit(solution)/shard_map/ppermute | solution.py:989
  13.7 8.6 %collective-permute-start.10 = (bf16[3,4,16,512]{3,2,0,1:T(8,128)(2,1)S(1)}, bf16[3,4,16,512]{3,2,0,1:T(8,128)(2,1)S(1)}, u32[]{:S(2)}, u32[]{:S(2)}) collective-permute-start(bf16[3,4,16,512]{3,2,0,1:T(8,128)(2,1)S(1)} %pad_maximum_fusion.7), channel_id=1, source_target_pairs={{0,6},{1,7},{2,4},{3,5},{4,2},{5,3},{6,0},{7,1},{8,14},{9,15},{10,... | collective-permute-start | bytes 589832 | tf_op jit(solution)/shard_map/ppermute | solution.py:989
  16.2 7.2 %collective-permute-start.9 = (bf16[3,4,16,512]{3,2,0,1:T(8,128)(2,1)S(1)}, bf16[3,4,16,512]{3,2,0,1:T(8,128)(2,1)S(1)}, u32[]{:S(2)}, u32[]{:S(2)}) collective-permute-start(bf16[3,4,16,512]{3,2,0,1:T(8,128)(2,1)S(1)} %pad_maximum_fusion.7), channel_id=1, source_target_pairs={{0,4},{1,5},{2,6},{3,7},{4,0},{5,1},{6,2},{7,3},{8,12},{9,13},{10,... | collective-permute-start | bytes 589832 | tf_op jit(solution)/shard_map/ppermute | solution.py:989
  16.7 6.8 %collective-permute-start.8 = (bf16[3,4,16,512]{3,2,0,1:T(8,128)(2,1)S(1)}, bf16[3,4,16,512]{3,2,0,1:T(8,128)(2,1)S(1)}, u32[]{:S(2)}, u32[]{:S(2)}) collective-permute-start(bf16[3,4,16,512]{3,2,0,1:T(8,128)(2,1)S(1)} %pad_maximum_fusion.7), channel_id=1, source_target_pairs={{0,2},{1,3},{2,0},{3,1},{4,6},{5,7},{6,4},{7,5},{8,10},{9,11},{10,... | collective-permute-start | bytes 589832 | tf_op jit(solution)/shard_map/ppermute | solution.py:989
  19.8 6.6 %collective-permute-start.4 = (bf16[5,2,16,512]{3,2,1,0:T(8,128)(2,1)S(1)}, bf16[5,2,16,512]{3,2,1,0:T(8,128)(2,1)S(1)}, u32[]{:S(2)}, u32[]{:S(2)}) collective-permute-start(bf16[5,2,16,512]{3,2,1,0:T(8,128)(2,1)S(1)} %pad_maximum_fusion.8), channel_id=1, source_target_pairs={{0,8},{1,9},{2,10},{3,11},{4,12},{5,13},{6,14},{7,15},{8,0},{9,1},... | collective-permute-start | bytes 491528 | tf_op jit(solution)/shard_map/ppermute | solution.py:989
  22.2 9.4 %collective-permute-start.13 = (bf16[2,144,512]{2,1,0:T(8,128)(2,1)S(1)}, bf16[2,144,512]{2,1,0:T(8,128)(2,1)S(1)}, u32[]{:S(2)}, u32[]{:S(2)}) collective-permute-start(bf16[2,144,512]{2,1,0:T(8,128)(2,1)S(1)} %pad_maximum_fusion.5), channel_id=1, source_target_pairs={{0,8},{1,9},{2,10},{3,11},{4,12},{5,13},{6,14},{7,15},{8,0},{9,1},... | collective-permute-start | bytes 884744 | tf_op jit(solution)/shard_map/ppermute | solution.py:989
  23.8 7.9 %collective-permute-start.11 = (bf16[3,4,4,16,512]{4,3,0,1,2:T(8,128)(2,1)S(1)}, bf16[3,4,4,16,512]{4,3,0,1,2:T(8,128)(2,1)S(1)}, u32[]{:S(2)}, u32[]{:S(2)}) collective-permute-start(bf16[3,4,4,16,512]{4,3,0,1,2:T(8,128)(2,1)S(1)} %pad_maximum_fusion.3), channel_id=1, source_target_pairs={{0,1},{1,0},{2,3},{3,2},{4,5},{5,4},{6,7},{7,6},{8,9},{9,8},{10,11... | collective-permute-start | bytes 2359304 | tf_op jit(solution)/shard_map/ppermute | solution.py:989
  26.5 20.8 %collective-permute-start.7 = (bf16[5,2,2,16,512]{4,3,2,1,0:T(8,128)(2,1)S(1)}, bf16[5,2,2,16,512]{4,3,2,1,0:T(8,128)(2,1)S(1)}, u32[]{:S(2)}, u32[]{:S(2)}) collective-permute-start(bf16[5,2,2,16,512]{4,3,2,1,0:T(8,128)(2,1)S(1)} %pad_maximum_fusion.4.rest_0_), channel_id=1, source_target_pairs={{0,6},{1,7},{2,4},{3,5},{4,2},{5,3},{6,0},{7,1},{8,14},{9,15},{10,... | collective-permute-start | bytes 983048 | tf_op jit(solution)/shard_map/ppermute | solution.py:989
  29.0 18.3 %collective-permute-start.6 = (bf16[5,2,2,16,512]{4,3,2,1,0:T(8,128)(2,1)S(1)}, bf16[5,2,2,16,512]{4,3,2,1,0:T(8,128)(2,1)S(1)}, u32[]{:S(2)}, u32[]{:S(2)}) collective-permute-start(bf16[5,2,2,16,512]{4,3,2,1,0:T(8,128)(2,1)S(1)} %pad_maximum_fusion.4.rest_0_), channel_id=1, source_target_pairs={{0,4},{1,5},{2,6},{3,7},{4,0},{5,1},{6,2},{7,3},{8,12},{9,13},{10,... | collective-permute-start | bytes 983048 | tf_op jit(solution)/shard_map/ppermute | solution.py:989
  29.5 17.8 %collective-permute-start.5 = (bf16[5,2,2,16,512]{4,3,2,1,0:T(8,128)(2,1)S(1)}, bf16[5,2,2,16,512]{4,3,2,1,0:T(8,128)(2,1)S(1)}, u32[]{:S(2)}, u32[]{:S(2)}) collective-permute-start(bf16[5,2,2,16,512]{4,3,2,1,0:T(8,128)(2,1)S(1)} %pad_maximum_fusion.4.rest_0_), channel_id=1, source_target_pairs={{0,2},{1,3},{2,0},{3,1},{4,6},{5,7},{6,4},{7,5},{8,10},{9,11},{10,... | collective-permute-start | bytes 983048 | tf_op jit(solution)/shard_map/ppermute | solution.py:989
  32.1 15.1 %copy-start = (bf16[3,4,4,2,16,512]{5,4,3,2,1,0:T(8,128)(2,1)}, bf16[3,4,4,2,16,512]{5,4,3,2,1,0:T(8,128)(2,1)S(1)}, u32[]{:S(2)}) copy-start(bf16[3,4,4,2,16,512]{5,4,3,2,1,0:T(8,128)(2,1)S(1)} %copy.37) | copy-start | bytes 4718596
  32.1 15.5 %collective-permute-start.15 = (bf16[2,2,64,512]{3,2,1,0:T(8,128)(2,1)S(1)}, bf16[2,2,64,512]{3,2,1,0:T(8,128)(2,1)S(1)}, u32[]{:S(2)}, u32[]{:S(2)}) collective-permute-start(bf16[2,2,64,512]{3,2,1,0:T(8,128)(2,1)S(1)} %pad_maximum_fusion.6.rest_2_.refs_0_), channel_id=1, source_target_pairs={{0,4},{1,5},{2,6},{3,7},{4,0},{5,1},{6,2},{7,3},{8,12},{9,13},{10,... | collective-permute-start | bytes 786440 | tf_op jit(solution)/shard_map/ppermute | solution.py:989
  33.7 15.3 %collective-permute-start.14 = (bf16[2,2,80,512]{3,2,1,0:T(8,128)(2,1)S(1)}, bf16[2,2,80,512]{3,2,1,0:T(8,128)(2,1)S(1)}, u32[]{:S(2)}, u32[]{:S(2)}) collective-permute-start(bf16[2,2,80,512]{3,2,1,0:T(8,128)(2,1)S(1)} %fusion.1.rest_1_.refs_0_), channel_id=1, source_target_pairs={{0,2},{1,3},{2,0},{3,1},{4,6},{5,7},{6,4},{7,5},{8,10},{9,11},{10,... | collective-permute-start | bytes 983048 | tf_op jit(solution)/shard_map/ppermute | solution.py:989
  49.0 3.8 %collective-permute-start.16 = (bf16[5,2,2,4,16,512]{5,4,2,1,0,3:T(8,128)(2,1)S(1)}, bf16[5,2,2,4,16,512]{5,4,2,1,0,3:T(8,128)(2,1)}, u32[]{:S(2)}, u32[]{:S(2)}) collective-permute-start(bf16[5,2,2,4,16,512]{5,4,2,1,0,3:T(8,128)(2,1)S(1)} %pad_maximum_fusion.2), channel_id=1, source_target_pairs={{0,1},{1,0},{2,3},{3,2},{4,5},{5,4},{6,7},{7,6},{8,9},{9,8},{10,11... | collective-permute-start | bytes 3932168 | tf_op jit(solution)/shard_map/ppermute | solution.py:989
  49.9 24.0 %collective-permute-start.20 = (bf16[2,2,2,64,512]{4,3,2,1,0:T(8,128)(2,1)}, bf16[2,2,2,64,512]{4,3,2,1,0:T(8,128)(2,1)}, u32[]{:S(2)}, u32[]{:S(2)}) collective-permute-start(bf16[2,2,2,64,512]{4,3,2,1,0:T(8,128)(2,1)} %place.3), channel_id=1, source_target_pairs={{0,1},{1,0},{2,3},{3,2},{4,5},{5,4},{6,7},{7,6},{8,9},{9,8},{10,11... | collective-permute-start | bytes 1572872 | tf_op jit(solution)/shard_map/ppermute | solution.py:989
  50.4 23.5 %collective-permute-start.18 = (bf16[2,2,2,64,512]{4,3,2,1,0:T(8,128)(2,1)}, bf16[2,2,2,64,512]{4,3,2,1,0:T(8,128)(2,1)}, u32[]{:S(2)}, u32[]{:S(2)}) collective-permute-start(bf16[2,2,2,64,512]{4,3,2,1,0:T(8,128)(2,1)} %place.3), channel_id=1, source_target_pairs={{0,2},{1,3},{2,0},{3,1},{4,6},{5,7},{6,4},{7,5},{8,10},{9,11},{10,... | collective-permute-start | bytes 1572872 | tf_op jit(solution)/shard_map/ppermute | solution.py:989
  51.3 22.7 %collective-permute-start.19 = (bf16[2,2,2,80,512]{4,3,2,1,0:T(8,128)(2,1)S(1)}, bf16[2,2,2,80,512]{4,3,2,1,0:T(8,128)(2,1)}, u32[]{:S(2)}, u32[]{:S(2)}) collective-permute-start(bf16[2,2,2,80,512]{4,3,2,1,0:T(8,128)(2,1)S(1)} %place.2), channel_id=1, source_target_pairs={{0,1},{1,0},{2,3},{3,2},{4,5},{5,4},{6,7},{7,6},{8,9},{9,8},{10,11... | collective-permute-start | bytes 1966088 | tf_op jit(solution)/shard_map/ppermute | solution.py:989
  51.4 22.6 %collective-permute-start.17 = (bf16[2,2,2,80,512]{4,3,2,1,0:T(8,128)(2,1)S(1)}, bf16[2,2,2,80,512]{4,3,2,1,0:T(8,128)(2,1)}, u32[]{:S(2)}, u32[]{:S(2)}) collective-permute-start(bf16[2,2,2,80,512]{4,3,2,1,0:T(8,128)(2,1)S(1)} %place.2), channel_id=1, source_target_pairs={{0,4},{1,5},{2,6},{3,7},{4,0},{5,1},{6,2},{7,3},{8,12},{9,13},{10,... | collective-permute-start | bytes 1966088 | tf_op jit(solution)/shard_map/ppermute | solution.py:989
  55.4 18.5 %copy-start.2 = (f32[6,512]{1,0:T(8,128)}, f32[6,512]{1,0:T(8,128)S(1)}, u32[]{:S(2)}) copy-start(f32[6,512]{1,0:T(8,128)S(1)} %reshape.261.norms_ref) | copy-start | bytes 36868
  74.0 4.0 %collective-permute-start.21 = (bf16[2,2,2,80,512]{4,3,2,1,0:T(8,128)(2,1)}, bf16[2,2,2,80,512]{4,3,2,1,0:T(8,128)(2,1)S(1)}, u32[]{:S(2)}, u32[]{:S(2)}) collective-permute-start(bf16[2,2,2,80,512]{4,3,2,1,0:T(8,128)(2,1)} %collective-permute-done.17), channel_id=1, source_target_pairs={{0,1},{1,0},{2,3},{3,2},{4,5},{5,4},{6,7},{7,6},{8,9},{9,8},{10,11... | collective-permute-start | bytes 1966088 | tf_op jit(solution)/shard_map/ppermute | solution.py:989
  75.3 2.7 %collective-permute-start.22 = (bf16[2,2,2,64,512]{4,3,2,1,0:T(8,128)(2,1)}, bf16[2,2,2,64,512]{4,3,2,1,0:T(8,128)(2,1)S(1)}, u32[]{:S(2)}, u32[]{:S(2)}) collective-permute-start(bf16[2,2,2,64,512]{4,3,2,1,0:T(8,128)(2,1)} %collective-permute-done.18), channel_id=1, source_target_pairs={{0,1},{1,0},{2,3},{3,2},{4,5},{5,4},{6,7},{7,6},{8,9},{9,8},{10,11... | collective-permute-start | bytes 1572872 | tf_op jit(solution)/shard_map/ppermute | solution.py:989
  108.1 9.5 %collective-permute-start.23 = (bf16[16,9,16,512]{3,2,1,0:T(8,128)(2,1)}, bf16[16,9,16,512]{3,2,1,0:T(8,128)(2,1)S(1)}, u32[]{:S(2)}, u32[]{:S(2)}) collective-permute-start(bf16[16,9,16,512]{3,2,1,0:T(8,128)(2,1)} %get-tuple-element.181), channel_id=1, source_target_pairs={{0,1},{1,0},{2,3},{3,2},{4,5},{5,4},{6,7},{7,6},{8,9},{9,8},{10,11... | collective-permute-start | bytes 7077896 | tf_op jit(solution)/shard_map/ppermute | solution.py:989
  108.6 9.0 %copy-start.9 = (bf16[16,9,16,512]{3,2,1,0:T(8,128)(2,1)S(1)}, bf16[16,9,16,512]{3,2,1,0:T(8,128)(2,1)}, u32[]{:S(2)}) copy-start(bf16[16,9,16,512]{3,2,1,0:T(8,128)(2,1)} %get-tuple-element.180) | copy-start | bytes 7077892
  118.8 19.4 %collective-permute-start.25 = (bf16[4,2,4,16,512]{4,3,2,1,0:T(8,128)(2,1)S(1)}, bf16[4,2,4,16,512]{4,3,2,1,0:T(8,128)(2,1)S(1)}, u32[]{:S(2)}, u32[]{:S(2)}) collective-permute-start(bf16[4,2,4,16,512]{4,3,2,1,0:T(8,128)(2,1)S(1)} %get-tuple-element.185.rest_1_), channel_id=1, source_target_pairs={{0,4},{1,5},{2,6},{3,7},{4,0},{5,1},{6,2},{7,3},{8,12},{9,13},{10,... | collective-permute-start | bytes 1572872 | tf_op jit(solution)/shard_map/ppermute | solution.py:989
  119.6 18.7 %collective-permute-start.24 = (bf16[4,2,5,16,512]{4,3,2,1,0:T(8,128)(2,1)S(1)}, bf16[4,2,5,16,512]{4,3,2,1,0:T(8,128)(2,1)S(1)}, u32[]{:S(2)}, u32[]{:S(2)}) collective-permute-start(bf16[4,2,5,16,512]{4,3,2,1,0:T(8,128)(2,1)S(1)} %get-tuple-element.184.rest_0_), channel_id=1, source_target_pairs={{0,2},{1,3},{2,0},{3,1},{4,6},{5,7},{6,4},{7,5},{8,10},{9,11},{10,... | collective-permute-start | bytes 1966088 | tf_op jit(solution)/shard_map/ppermute | solution.py:989
  139.2 13.6 %collective-permute-start.27 = (bf16[4,4,16,512]{3,2,1,0:T(8,128)(2,1)S(1)}, bf16[4,4,16,512]{3,2,1,0:T(8,128)(2,1)S(1)}, u32[]{:S(2)}, u32[]{:S(2)}) collective-permute-start(bf16[4,4,16,512]{3,2,1,0:T(8,128)(2,1)S(1)} %get-tuple-element.202.rest_1_), channel_id=1, source_target_pairs={{0,2},{1,3},{2,0},{3,1},{4,6},{5,7},{6,4},{7,5},{8,10},{9,11},{10,... | collective-permute-start | bytes 786440 | tf_op jit(solution)/shard_map/ppermute | solution.py:989
  141.1 11.6 %collective-permute-start.26 = (bf16[4,5,16,512]{3,2,1,0:T(8,128)(2,1)S(1)}, bf16[4,5,16,512]{3,2,1,0:T(8,128)(2,1)S(1)}, u32[]{:S(2)}, u32[]{:S(2)}) collective-permute-start(bf16[4,5,16,512]{3,2,1,0:T(8,128)(2,1)S(1)} %get-tuple-element.201.rest_0_), channel_id=1, source_target_pairs={{0,4},{1,5},{2,6},{3,7},{4,0},{5,1},{6,2},{7,3},{8,12},{9,13},{10,... | collective-permute-start | bytes 983048 | tf_op jit(solution)/shard_map/ppermute | solution.py:989
  153.0 4.5 %collective-permute-start.28 = (bf16[16,5,16,512]{3,2,1,0:T(8,128)(2,1)S(1)}, bf16[16,5,16,512]{3,2,1,0:T(8,128)(2,1)S(1)}, u32[]{:S(2)}, u32[]{:S(2)}) collective-permute-start(bf16[16,5,16,512]{3,2,1,0:T(8,128)(2,1)S(1)} %get-tuple-element.214), channel_id=1, source_target_pairs={{0,1},{1,0},{2,3},{3,2},{4,5},{5,4},{6,7},{7,6},{8,9},{9,8},{10,11... | collective-permute-start | bytes 3932168 | tf_op jit(solution)/shard_map/ppermute | solution.py:989
  153.4 23.5 %collective-permute-start.32 = (bf16[2,9,16,512]{3,2,1,0:T(8,128)(2,1)S(1)}, bf16[2,9,16,512]{3,2,1,0:T(8,128)(2,1)S(1)}, u32[]{:S(2)}, u32[]{:S(2)}) collective-permute-start(bf16[2,9,16,512]{3,2,1,0:T(8,128)(2,1)S(1)} %get-tuple-element.210.rest_0_), channel_id=1, source_target_pairs={{0,8},{1,9},{2,10},{3,11},{4,12},{5,13},{6,14},{7,15},{8,0},{9,1},... | collective-permute-start | bytes 884744 | tf_op jit(solution)/shard_map/ppermute | solution.py:989
  157.9 19.1 %collective-permute-start.29 = (bf16[4,5,16,512]{3,2,1,0:T(8,128)(2,1)S(1)}, bf16[4,5,16,512]{3,2,1,0:T(8,128)(2,1)S(1)}, u32[]{:S(2)}, u32[]{:S(2)}) collective-permute-start(bf16[4,5,16,512]{3,2,1,0:T(8,128)(2,1)S(1)} %get-tuple-element.215.rest_1_), channel_id=1, source_target_pairs={{0,2},{1,3},{2,0},{3,1},{4,6},{5,7},{6,4},{7,5},{8,10},{9,11},{10,... | collective-permute-start | bytes 983048 | tf_op jit(solution)/shard_map/ppermute | solution.py:989
  158.5 18.5 %collective-permute-start.30 = (bf16[4,5,16,512]{3,2,1,0:T(8,128)(2,1)S(1)}, bf16[4,5,16,512]{3,2,1,0:T(8,128)(2,1)S(1)}, u32[]{:S(2)}, u32[]{:S(2)}) collective-permute-start(bf16[4,5,16,512]{3,2,1,0:T(8,128)(2,1)S(1)} %get-tuple-element.216.rest_2_), channel_id=1, source_target_pairs={{0,4},{1,5},{2,6},{3,7},{4,0},{5,1},{6,2},{7,3},{8,12},{9,13},{10,... | collective-permute-start | bytes 983048 | tf_op jit(solution)/shard_map/ppermute | solution.py:989
  160.5 16.5 %collective-permute-start.31 = (bf16[4,5,16,512]{3,2,1,0:T(8,128)(2,1)S(1)}, bf16[4,5,16,512]{3,2,1,0:T(8,128)(2,1)S(1)}, u32[]{:S(2)}, u32[]{:S(2)}) collective-permute-start(bf16[4,5,16,512]{3,2,1,0:T(8,128)(2,1)S(1)} %get-tuple-element.217.rest_3_), channel_id=1, source_target_pairs={{0,6},{1,7},{2,4},{3,5},{4,2},{5,3},{6,0},{7,1},{8,14},{9,15},{10,... | collective-permute-start | bytes 983048 | tf_op jit(solution)/shard_map/ppermute | solution.py:989
  177.3 2.9 %collective-permute-start.33 = (bf16[16,3,16,512]{3,2,1,0:T(8,128)(2,1)S(1)}, bf16[16,3,16,512]{3,2,1,0:T(8,128)(2,1)S(1)}, u32[]{:S(2)}, u32[]{:S(2)}) collective-permute-start(bf16[16,3,16,512]{3,2,1,0:T(8,128)(2,1)S(1)} %get-tuple-element.230), channel_id=1, source_target_pairs={{0,1},{1,0},{2,3},{3,2},{4,5},{5,4},{6,7},{7,6},{8,9},{9,8},{10,11... | collective-permute-start | bytes 2359304 | tf_op jit(solution)/shard_map/ppermute | solution.py:989
  177.3 17.4 %collective-permute-start.42 = (bf16[1,9,16,512]{3,2,1,0:T(8,128)(2,1)S(1)}, bf16[1,9,16,512]{3,2,1,0:T(8,128)(2,1)S(1)}, u32[]{:S(2)}, u32[]{:S(2)}) collective-permute-start(bf16[1,9,16,512]{3,2,1,0:T(8,128)(2,1)S(1)} %get-tuple-element.228), channel_id=1, source_target_pairs={{0,16},{1,17},{2,18},{3,19},{4,20},{5,21},{6,22},{7,23},{8,24},{9,... | collective-permute-start | bytes 442376 | tf_op jit(solution)/shard_map/ppermute | solution.py:989
  179.8 8.2 %collective-permute-start.40 = (bf16[2,5,16,512]{3,2,1,0:T(8,128)(2,1)S(1)}, bf16[2,5,16,512]{3,2,1,0:T(8,128)(2,1)S(1)}, u32[]{:S(2)}, u32[]{:S(2)}) collective-permute-start(bf16[2,5,16,512]{3,2,1,0:T(8,128)(2,1)S(1)} %get-tuple-element.225), channel_id=1, source_target_pairs={{0,8},{1,9},{2,10},{3,11},{4,12},{5,13},{6,14},{7,15},{8,0},{9,1},... | collective-permute-start | bytes 491528 | tf_op jit(solution)/shard_map/ppermute | solution.py:989
  180.4 10.4 %collective-permute-start.34 = (bf16[4,3,16,512]{3,2,1,0:T(8,128)(2,1)S(1)}, bf16[4,3,16,512]{3,2,1,0:T(8,128)(2,1)S(1)}, u32[]{:S(2)}, u32[]{:S(2)}) collective-permute-start(bf16[4,3,16,512]{3,2,1,0:T(8,128)(2,1)S(1)} %get-tuple-element.232), channel_id=1, source_target_pairs={{0,2},{1,3},{2,0},{3,1},{4,6},{5,7},{6,4},{7,5},{8,10},{9,11},{10,... | collective-permute-start | bytes 589832 | tf_op jit(solution)/shard_map/ppermute | solution.py:989
  181.3 11.0 %collective-permute-start.35 = (bf16[4,3,16,512]{3,2,1,0:T(8,128)(2,1)S(1)}, bf16[4,3,16,512]{3,2,1,0:T(8,128)(2,1)S(1)}, u32[]{:S(2)}, u32[]{:S(2)}) collective-permute-start(bf16[4,3,16,512]{3,2,1,0:T(8,128)(2,1)S(1)} %get-tuple-element.233), channel_id=1, source_target_pairs={{0,4},{1,5},{2,6},{3,7},{4,0},{5,1},{6,2},{7,3},{8,12},{9,13},{10,... | collective-permute-start | bytes 589832 | tf_op jit(solution)/shard_map/ppermute | solution.py:989
  183.3 9.1 %collective-permute-start.36 = (bf16[4,3,16,512]{3,2,1,0:T(8,128)(2,1)S(1)}, bf16[4,3,16,512]{3,2,1,0:T(8,128)(2,1)S(1)}, u32[]{:S(2)}, u32[]{:S(2)}) collective-permute-start(bf16[4,3,16,512]{3,2,1,0:T(8,128)(2,1)S(1)} %get-tuple-element.234), channel_id=1, source_target_pairs={{0,6},{1,7},{2,4},{3,5},{4,2},{5,3},{6,0},{7,1},{8,14},{9,15},{10,... | collective-permute-start | bytes 589832 | tf_op jit(solution)/shard_map/ppermute | solution.py:989
  188.1 7.2 %collective-permute-start.41 = (bf16[1,5,16,512]{3,2,1,0:T(8,128)(2,1)S(1)}, bf16[1,5,16,512]{3,2,1,0:T(8,128)(2,1)S(1)}, u32[]{:S(2)}, u32[]{:S(2)}) collective-permute-start(bf16[1,5,16,512]{3,2,1,0:T(8,128)(2,1)S(1)} %get-tuple-element.244), channel_id=1, source_target_pairs={{0,16},{1,17},{2,18},{3,19},{4,20},{5,21},{6,22},{7,23},{8,24},{9,... | collective-permute-start | bytes 245768 | tf_op jit(solution)/shard_map/ppermute | solution.py:989
  192.5 10.4 %collective-permute-start.37 = (bf16[1,3,16,512]{3,2,1,0:T(8,128)(2,1)S(1)}, bf16[1,3,16,512]{3,2,1,0:T(8,128)(2,1)S(1)}, u32[]{:S(2)}, u32[]{:S(2)}) collective-permute-start(bf16[1,3,16,512]{3,2,1,0:T(8,128)(2,1)S(1)} %get-tuple-element.236), channel_id=1, source_target_pairs={{0,8},{1,9},{2,10},{3,11},{4,12},{5,13},{6,14},{7,15},{8,0},{9,1},... | collective-permute-start | bytes 147464 | tf_op jit(solution)/shard_map/ppermute | solution.py:989
  195.9 5.6 %collective-permute-start.38 = (bf16[1,3,16,512]{3,2,1,0:T(8,128)(2,1)S(1)}, bf16[1,3,16,512]{3,2,1,0:T(8,128)(2,1)S(1)}, u32[]{:S(2)}, u32[]{:S(2)}) collective-permute-start(bf16[1,3,16,512]{3,2,1,0:T(8,128)(2,1)S(1)} %get-tuple-element.237), channel_id=1, source_target_pairs={{0,16},{1,17},{2,18},{3,19},{4,20},{5,21},{6,22},{7,23},{8,24},{9,... | collective-permute-start | bytes 147464 | tf_op jit(solution)/shard_map/ppermute | solution.py:989
  196.9 6.0 %collective-permute-start.39 = (bf16[1,3,16,512]{3,2,1,0:T(8,128)(2,1)S(1)}, bf16[1,3,16,512]{3,2,1,0:T(8,128)(2,1)S(1)}, u32[]{:S(2)}, u32[]{:S(2)}) collective-permute-start(bf16[1,3,16,512]{3,2,1,0:T(8,128)(2,1)S(1)} %get-tuple-element.238), channel_id=1, source_target_pairs={{0,24},{1,25},{2,26},{3,27},{4,28},{5,29},{6,30},{7,31},{8,16},{9,... | collective-permute-start | bytes 147464 | tf_op jit(solution)/shard_map/ppermute | solution.py:989
  (15 other events, 55.9 us)
where the time goes:
time: 205 us; the launch traced here: 204 us
  Pallas kernels  124 us (60%)
  starting transfers between devices  50.2 us (24%)
  waiting for transfers between devices  21.9 us (11%)
  local copies, waits for them, and re-layouts  3.14 us (2%)
  other arithmetic  3.09 us (2%)
    ppermute x43, starting transfers between devices, swap(): lax.ppermute(x, ('dp', 'fsdp'), [(i, i ^ mask) for i in range(mesh_size())])  50.2 us
    pallas_call x1, Pallas kernels, ffn(): pl.pallas_call(ffn_kernel, grid=(total // rows,), in_specs=[smem, smem] +...  29.1 us
    pallas_call x2, Pallas kernels, cross_backward(): pl.pallas_call(functools.partial(cross_backward_kernel, tile, block, firs...  27.4 us
    ppermute x43, waiting for transfers between devices, swap(): lax.ppermute(x, ('dp', 'fsdp'), [(i, i ^ mask) for i in range(mesh_size())])  21.9 us
    pallas_call x1, Pallas kernels, cross_forward(): pl.pallas_call(functools.partial(cross_forward_kernel, tile, block), grid...  18.5 us
    pallas_call x1, Pallas kernels, self_backward(): pl.pallas_call(functools.partial(self_backward_kernel, tile, block), grid...  15.4 us
    pallas_call x1, Pallas kernels, self_forward(): pl.pallas_call(functools.partial(self_forward_kernel, tile, block), grid_...  12.1 us
    pallas_call x1, Pallas kernels, between(): pl.pallas_call(between_kernel, grid=(total // rows,), in_specs=[pl.BlockS...  6.68 us
  transfers between devices with their start and end apart: 43, of which 15 were waited for; matrix products, arithmetic and copies ran while one was open for 3% of the time, Pallas kernels for 45%

commit v1 on v0

--- a/solution.py
+++ b/solution.py
@@ -259,7 +259,7 @@
         ),
         out_shape=[full] * 4 + [sds((total, LANES), f32)],
         name="self_forward",
-        **params(13, 32),
+        **params(13, 26),
     )(items, *placed(x), weights, weights, weights, idr, *after)
 
 
@@ -342,7 +342,7 @@
             sds((total, width), bf16), sds((total, width), f32), sds((total, width), bf16), sds((total, LANES), f32),
         ],
         name="cross_forward",
-        **params(19, 44),
+        **params(19, 38),
     )(items, *placed(memory), weights, weights, *placed(x, o1), weights, weights, norms, idr, idk, *after)
 
 
@@ -504,7 +504,7 @@
         scratch_shapes=[pltpu.VMEM((width, blocks * width), f32), pltpu.VMEM((blocks * width, width), f32), pltpu.VMEM((width, width), f32)]
         + ([pltpu.VMEM(h, bf16) for h in held] if devices > 1 else []),
         name="ffn",
-        **params(32, 56),
+        **params(32, 43),
     )(core, here, *placed(h1, x, cot, o2), norms, *weights)
 
 
@@ -720,7 +720,7 @@
         ),
         out_shape=[sds((total, width), bf16), side, side],
         name="self_backward",
-        **params(17, 34),
+        **params(17, 26),
     )(core, items, q, k, v, do, l, delta, idr, x, weights, weights, weights, sofar, *after)
 
 
@@ -1163,6 +1163,7 @@
     keep, send = tie((keep, send), two[1], one[1])
     three = [keep, send] if whole_tiles else resplit(keep, send, devices, core[0], 3)
     three = next_pieces(swap_pieces(three, groups[0]), groups, 1)
+    early_three = three[1]
     for i in range(2, len(groups)):
         three = next_pieces(swap_pieces(three, groups[i - 1]), groups, i)
     for i in range(3, len(single)):
@@ -1173,7 +1174,7 @@
     def flat(g):
         return g.reshape(-1)
 
-    chains = [swap_pieces(one, single[-1], [three[1]]), swap_pieces(two, single[-1], [three[1]]), swap_pieces(three, groups[-1])]
+    chains = [swap_pieces(one, single[-1], [early_three]), swap_pieces(two, single[-1], [three[1]]), swap_pieces(three, groups[-1])]
     chains = [[p.reshape(-1, own_rows, width) for p in chain] for chain in chains]
     if whole_tiles:
         lane_rows = size // LANES

time: 205 us -> 201 us (0.980)
    pallas_call x1, Pallas kernels: 29.1 us -> 27 us  [ffn(): pl.pallas_call(ffn_kernel, grid=(total // rows,), in_specs=[smem, smem] +...]
  transfers between devices with their start and end apart: 43 -> 43, of which waited for: 15 -> 16; matrix products, arithmetic and copies ran while one was open for 3% -> 3% of each run, Pallas kernels for 45% -> 46%
where the time goes in v1:
time: 201 us; the launch traced here: 200 us
  Pallas kernels  122 us (61%)
  starting transfers between devices  50.9 us (25%)
  waiting for transfers between devices  20.5 us (10%)
  other arithmetic  3.09 us (2%)
  local copies, waits for them, and re-layouts  2.09 us (1%)
    ppermute x43, starting transfers between devices, swap(): lax.ppermute(x, ('dp', 'fsdp'), [(i, i ^ mask) for i in range(mesh_size())])  50.9 us
    pallas_call x2, Pallas kernels, cross_backward(): pl.pallas_call(functools.partial(cross_backward_kernel, tile, block, firs...  27.3 us
    pallas_call x1, Pallas kernels, ffn(): pl.pallas_call(ffn_kernel, grid=(total // rows,), in_specs=[smem, smem] +...  27 us
    ppermute x43, waiting for transfers between devices, swap(): lax.ppermute(x, ('dp', 'fsdp'), [(i, i ^ mask) for i in range(mesh_size())])  20.5 us
    pallas_call x1, Pallas kernels, cross_forward(): pl.pallas_call(functools.partial(cross_forward_kernel, tile, block), grid...  18.4 us
    pallas_call x1, Pallas kernels, self_backward(): pl.pallas_call(functools.partial(self_backward_kernel, tile, block), grid...  15.9 us
    pallas_call x1, Pallas kernels, self_forward(): pl.pallas_call(functools.partial(self_forward_kernel, tile, block), grid_...  12 us
    pallas_call x1, Pallas kernels, between(): pl.pallas_call(between_kernel, grid=(total // rows,), in_specs=[pl.BlockS...  6.66 us
  transfers between devices with their start and end apart: 43, of which 16 were waited for; matrix products, arithmetic and copies ran while one was open for 3% of the time, Pallas kernels for 46%

profile of v1, /device:TPU:0, one launch (start us, length us, event | category | flops | bytes accessed | tf_op | source)
XLA Modules:
  0.0 199.7 jit_solution(5489959929076632195)
XLA Ops:
  1.4 3.1 %collective-permute-start.2 = (bf16[3,16,512]{2,1,0:T(8,128)(2,1)S(1)}, bf16[3,16,512]{2,1,0:T(8,128)(2,1)S(1)}, u32[]{:S(2)}, u32[]{:S(2)}) collective-permute-start(bf16[3,16,512]{2,1,0:T(8,128)(2,1)S(1)} %pack_self.1), channel_id=1, source_target_pairs={{0,8},{1,9},{2,10},{3,11},{4,12},{5,13},{6,14},{7,15},{8,0},{9,1},... | collective-permute-start | bytes 147464 | tf_op jit(solution)/shard_map/ppermute | solution.py:989
  4.5 2.6 %collective-permute-start.1 = (bf16[3,16,512]{2,1,0:T(8,128)(2,1)S(1)}, bf16[3,16,512]{2,1,0:T(8,128)(2,1)S(1)}, u32[]{:S(2)}, u32[]{:S(2)}) collective-permute-start(bf16[3,16,512]{2,1,0:T(8,128)(2,1)S(1)} %pack_self.1), channel_id=1, source_target_pairs={{0,16},{1,17},{2,18},{3,19},{4,20},{5,21},{6,22},{7,23},{8,24},{9,... | collective-permute-start | bytes 147464 | tf_op jit(solution)/shard_map/ppermute | solution.py:989
  7.8 0.8 pack_cross.1
  8.6 2.0 collective-permute-start.3
  10.5 1.0 pack_ffn.1
  11.5 1.1 collective-permute-start.12
  12.6 1.0 collective-permute-done
  13.7 2.5 %collective-permute-start.10 = (bf16[3,4,16,512]{3,2,0,1:T(8,128)(2,1)S(1)}, bf16[3,4,16,512]{3,2,0,1:T(8,128)(2,1)S(1)}, u32[]{:S(2)}, u32[]{:S(2)}) collective-permute-start(bf16[3,4,16,512]{3,2,0,1:T(8,128)(2,1)S(1)} %pad_maximum_fusion.7), channel_id=1, source_target_pairs={{0,6},{1,7},{2,4},{3,5},{4,2},{5,3},{6,0},{7,1},{8,14},{9,15},{10,... | collective-permute-start | bytes 589832 | tf_op jit(solution)/shard_map/ppermute | solution.py:989
  17.2 2.2 %plan.1 = (s32[1,1024]{1,0:T(1,128)S(1)}, s32[1,2048]{1,0:T(1,128)S(1)}, s32[3,36]{1,0:T(4,128)S(1)}, s32[3,68]{1,0:T(4,128)S(1)}) custom-call(s32[1,16]{1,0:T(1,128)S(1)} %copy-done.3, s32[1,17]{1,0:T(1,128)S(1)} %copy-done.4), custom_call_target="tpu_custom_call" | custom-call | flops 1000000000 | bytes 1048576 | tf_op jit(solution)/shard_map/plan/pallas_call | solution.py:956
  20.1 2.0 collective-permute-done.12
  22.2 1.1 collective-permute-done.9
  23.8 2.6 %collective-permute-done.4 = bf16[5,2,16,512]{3,2,1,0:T(8,128)(2,1)S(1)} collective-permute-done((bf16[5,2,16,512]{3,2,1,0:T(8,128)(2,1)S(1)}, bf16[5,2,16,512]{3,2,1,0:T(8,128)(2,1)S(1)}, u32[]{:S(2)}, u32[]{:S(2)}) %collective-permute-start.4) | collective-permute-done | bytes 163872 | tf_op jit(solution)/shard_map/ppermute | solution.py:989
  26.5 2.5 %collective-permute-start.7 = (bf16[5,2,2,16,512]{4,3,2,1,0:T(8,128)(2,1)S(1)}, bf16[5,2,2,16,512]{4,3,2,1,0:T(8,128)(2,1)S(1)}, u32[]{:S(2)}, u32[]{:S(2)}) collective-permute-start(bf16[5,2,2,16,512]{4,3,2,1,0:T(8,128)(2,1)S(1)} %pad_maximum_fusion.4.rest_0_), channel_id=1, source_target_pairs={{0,6},{1,7},{2,4},{3,5},{4,2},{5,3},{6,0},{7,1},{8,14},{9,15},{10,... | collective-permute-start | bytes 983048 | tf_op jit(solution)/shard_map/ppermute | solution.py:989
  30.0 1.5 collective-permute-done.13
  32.1 1.6 collective-permute-start.15
  33.7 1.5 collective-permute-start.14
  35.2 12.0 %self_forward.1 = (bf16[1024,512]{1,0:T(8,128)(2,1)}, bf16[1024,512]{1,0:T(8,128)(2,1)}, bf16[1024,512]{1,0:T(8,128)(2,1)}, bf16[1024,512]{1,0:T(8,128)(2,1)}, f32[1024,128]{1,0:T(8,128)}) custom-call(s32[3,36]{1,0:T(4,128)S(1)} %get-tuple-element.143.items_ref, bf16[1024,512]{1,0:T(8,128)(2,1)} %x_ref.7, bf16[3,512,512]{2,1,0:T(8,128)(2,1)S(1)} %bitcast.136, ...), custom_call_target="tpu_custom_call" | custom-call | flops 12999999488 | bytes 1048576 | tf_op jit(solution)/shard_map/self_forward/pallas_call | solution.py:247
  47.6 1.4 collective-permute-done.14.refs_1_
  49.1 0.8 place.3
  51.4 1.4 collective-permute-start.17
  52.8 1.5 select_bitcast_fusion.1
  55.4 18.4 %cross_forward.1 = (bf16[2048,512]{1,0:T(8,128)(2,1)}, bf16[2048,512]{1,0:T(8,128)(2,1)}, bf16[1024,512]{1,0:T(8,128)(2,1)}, bf16[1024,512]{1,0:T(8,128)(2,1)}, ...) custom-call(s32[3,68]{1,0:T(4,128)S(1)} %get-tuple-element.137.items_ref, ...), custom_call_target="tpu_custom_call" | custom-call | flops 19000000512 | bytes 1048576 | tf_op jit(solution)/shard_map/cross_forward/pallas_call | solution.py:321
  74.4 2.5 %collective-permute-done.22 = bf16[2,2,2,64,512]{4,3,2,1,0:T(8,128)(2,1)S(1)} collective-permute-done((bf16[2,2,2,64,512]{4,3,2,1,0:T(8,128)(2,1)}, bf16[2,2,2,64,512]{4,3,2,1,0:T(8,128)(2,1)S(1)}, u32[]{:S(2)}, u32[]{:S(2)}) %collective-permute-start.22) | collective-permute-done | bytes 524320 | tf_op jit(solution)/shard_map/ppermute | solution.py:989
  77.0 27.0 %ffn.1 = (bf16[1024,512]{1,0:T(8,128)(2,1)}, bf16[1024,512]{1,0:T(8,128)(2,1)}, bf16[1024,512]{1,0:T(8,128)(2,1)}, bf16[1024,512]{1,0:T(8,128)(2,1)}, f32[1024,1...) custom-call(s32[1]{0:T(128)} %bitcast.core_ref, ...), custom_call_target="tpu_custom_call" | custom-call | flops 32000000000 | bytes 1048576 | tf_op jit(solution)/shard_map/ffn/pallas_call | solution.py:495
  104.2 8.8 %cross_backward.2 = (bf16[1024,128]{1,0:T(8,128)(2,1)S(1)}, bf16[2048,128]{1,0:T(8,128)(2,1)S(1)}, bf16[2048,128]{1,0:T(8,128)(2,1)S(1)}, bf16[2,512,128]{2,1,0:T(8,128)(2,1)S(1)}) custom-call(s32[3,68]{1,0:T(4,128)S(1)} %get-tuple-element.137.items_ref, bf16[1024,512]{1,0:T(8,128)(2,1)} %get-tuple-element.174.q2_ref, ...), custom_call_target="tpu_custom_call" | custom-call | flops 8999999488 | bytes 1048576 | tf_op jit(solution)/shard_map/cross_backward/pallas_call | solution.py:558
  113.0 1.2 first_pair.1
  114.2 2.9 %collective-permute-start.25 = (bf16[4,2,4,16,512]{4,3,2,1,0:T(8,128)(2,1)S(1)}, bf16[4,2,4,16,512]{4,3,2,1,0:T(8,128)(2,1)S(1)}, u32[]{:S(2)}, u32[]{:S(2)}) collective-permute-start(bf16[4,2,4,16,512]{4,3,2,1,0:T(8,128)(2,1)S(1)} %get-tuple-element.185.rest_1_), channel_id=1, source_target_pairs={{0,4},{1,5},{2,6},{3,7},{4,0},{5,1},{6,2},{7,3},{8,12},{9,13},{10,... | collective-permute-start | bytes 1572872 | tf_op jit(solution)/shard_map/ppermute | solution.py:989
  117.1 18.5 %cross_backward.3 = (bf16[1024,384]{1,0:T(8,128)(2,1)S(1)}, bf16[2048,384]{1,0:T(8,128)(2,1)S(1)}, bf16[2048,384]{1,0:T(8,128)(2,1)S(1)}, bf16[2,512,384]{2,1,0:T(8,128)(2,1)S(1)}) custom-call(s32[3,68]{1,0:T(4,128)S(1)} %get-tuple-element.137.items_ref, bf16[1024,512]{1,0:T(8,128)(2,1)} %get-tuple-element.174.q2_ref, ...), custom_call_target="tpu_custom_call" | custom-call | flops 19000000512 | bytes 1048576 | tf_op jit(solution)/shard_map/cross_backward/pallas_call | solution.py:558
  135.6 0.9 second_pair.1
  136.5 3.4 %collective-permute-start.27 = (bf16[4,4,16,512]{3,2,1,0:T(8,128)(2,1)S(1)}, bf16[4,4,16,512]{3,2,1,0:T(8,128)(2,1)S(1)}, u32[]{:S(2)}, u32[]{:S(2)}) collective-permute-start(bf16[4,4,16,512]{3,2,1,0:T(8,128)(2,1)S(1)} %get-tuple-element.202.rest_1_), channel_id=1, source_target_pairs={{0,2},{1,3},{2,0},{3,1},{4,6},{5,7},{6,4},{7,5},{8,10},{9,11},{10,... | collective-permute-start | bytes 786440 | tf_op jit(solution)/shard_map/ppermute | solution.py:989
  140.0 3.6 %memory_grad.1.rest_0_ = bf16[2048,512]{1,0:T(8,128)(2,1)} custom-call(bf16[2048,128]{1,0:T(8,128)(2,1)S(1)} %get-tuple-element.193.ka_ref, bf16[2048,384]{1,0:T(8,128)(2,1)S(1)} %get-tuple-element.194.kb_ref, bf16[2048,128]{1,0:T(8,128)(2,1)S(1)} %get-tuple-element.195.va_ref, bf16[2048,384]{1,0:T(8,128)(2,1)S(1)} %get-tuple-element.196.vb_ref, ...), custom_call_target="tpu_custom_call" | custom-call | flops 4000000000 | bytes 1048576 | tf_op jit(solution)/shard_map/memory_grad/pallas_call | solution.py:586
  143.6 6.7 %between.1 = (bf16[1024,512]{1,0:T(8,128)(2,1)S(1)}, bf16[1024,512]{1,0:T(8,128)(2,1)S(1)}, f32[1024,128]{1,0:T(8,128)S(1)}, bf16[16,5,16,512]{3,2,1,0:T(8,128)(...) custom-call(s32[1]{0:T(128)} %bitcast.core_ref, bf16[2,512,128]{2,1,0:T(8,128)(2,1)S(1)} %get-tuple-element.179.ga_ref, ...), custom_call_target="tpu_custom_call" | custom-call | flops 7000000000 | bytes 1048576 | tf_op jit(solution)/shard_map/between/pallas_call | solution.py:645
  150.5 2.8 %collective-permute-start.32 = (bf16[2,9,16,512]{3,2,1,0:T(8,128)(2,1)S(1)}, bf16[2,9,16,512]{3,2,1,0:T(8,128)(2,1)S(1)}, u32[]{:S(2)}, u32[]{:S(2)}) collective-permute-start(bf16[2,9,16,512]{3,2,1,0:T(8,128)(2,1)S(1)} %get-tuple-element.210.rest_0_), channel_id=1, source_target_pairs={{0,8},{1,9},{2,10},{3,11},{4,12},{5,13},{6,14},{7,15},{8,0},{9,1},... | collective-permute-start | bytes 884744 | tf_op jit(solution)/shard_map/ppermute | solution.py:989
  154.0 1.9 collective-permute-start.29
  156.1 1.4 collective-permute-start.31
  157.5 15.9 %self_backward.1 = (bf16[1024,512]{1,0:T(8,128)(2,1)}, bf16[16,3,16,512]{3,2,1,0:T(8,128)(2,1)S(1)}, bf16[16,3,16,512]{3,2,1,0:T(8,128)(2,1)S(1)}) custom-call(s32[1]{0:T(128)} %bitcast.core_ref, s32[3,36]{1,0:T(4,128)S(1)} %get-tuple-element.143.items_ref, bf16[1024,512]{1,0:T(8,128)(2,1)S(1)} %copy-done.7, bf16[1024,512]{1,0:T(8,128)(2,1)S(1)} %copy-done.8, ...), custom_call_target="tpu_custom_call" | custom-call | flops 16999999488 | bytes 1048576 | tf_op jit(solution)/shard_map/self_backward/pallas_call | solution.py:707
  173.9 1.2 collective-permute-start.42
  175.2 2.8 %collective-permute-start.40 = (bf16[2,5,16,512]{3,2,1,0:T(8,128)(2,1)S(1)}, bf16[2,5,16,512]{3,2,1,0:T(8,128)(2,1)S(1)}, u32[]{:S(2)}, u32[]{:S(2)}) collective-permute-start(bf16[2,5,16,512]{3,2,1,0:T(8,128)(2,1)S(1)} %get-tuple-element.225), channel_id=1, source_target_pairs={{0,8},{1,9},{2,10},{3,11},{4,12},{5,13},{6,14},{7,15},{8,0},{9,1},... | collective-permute-start | bytes 491528 | tf_op jit(solution)/shard_map/ppermute | solution.py:989
  178.2 1.5 collective-permute-start.35
  180.3 1.5 collective-permute-start.34
  181.8 2.8 %collective-permute-done.40 = bf16[2,5,16,512]{3,2,1,0:T(8,128)(2,1)S(1)} collective-permute-done((bf16[2,5,16,512]{3,2,1,0:T(8,128)(2,1)S(1)}, bf16[2,5,16,512]{3,2,1,0:T(8,128)(2,1)S(1)}, u32[]{:S(2)}, u32[]{:S(2)}) %collective-permute-start.40) | collective-permute-done | bytes 163872 | tf_op jit(solution)/shard_map/ppermute | solution.py:989
  184.6 2.9 %collective-permute-start.41 = (bf16[1,5,16,512]{3,2,1,0:T(8,128)(2,1)S(1)}, bf16[1,5,16,512]{3,2,1,0:T(8,128)(2,1)S(1)}, u32[]{:S(2)}, u32[]{:S(2)}) collective-permute-start(bf16[1,5,16,512]{3,2,1,0:T(8,128)(2,1)S(1)} %get-tuple-element.244), channel_id=1, source_target_pairs={{0,16},{1,17},{2,18},{3,19},{4,20},{5,21},{6,22},{7,23},{8,24},{9,... | collective-permute-start | bytes 245768 | tf_op jit(solution)/shard_map/ppermute | solution.py:989
  188.3 1.0 collective-permute-done.35
  189.2 1.2 collective-permute-done.34
  190.5 1.3 collective-permute-start.37
  191.8 1.3 collective-permute-start.38
  193.1 2.0 %collective-permute-start.39 = (bf16[1,3,16,512]{3,2,1,0:T(8,128)(2,1)S(1)}, bf16[1,3,16,512]{3,2,1,0:T(8,128)(2,1)S(1)}, u32[]{:S(2)}, u32[]{:S(2)}) collective-permute-start(bf16[1,3,16,512]{3,2,1,0:T(8,128)(2,1)S(1)} %get-tuple-element.238), channel_id=1, source_target_pairs={{0,24},{1,25},{2,26},{3,27},{4,28},{5,29},{6,30},{7,31},{8,16},{9,... | collective-permute-start | bytes 147464 | tf_op jit(solution)/shard_map/ppermute | solution.py:989
  196.3 2.0 %collective-permute-done.38 = bf16[1,3,16,512]{3,2,1,0:T(8,128)(2,1)S(1)} collective-permute-done((bf16[1,3,16,512]{3,2,1,0:T(8,128)(2,1)S(1)}, bf16[1,3,16,512]{3,2,1,0:T(8,128)(2,1)S(1)}, u32[]{:S(2)}, u32[]{:S(2)}) %collective-permute-start.38) | collective-permute-done | bytes 49184 | tf_op jit(solution)/shard_map/ppermute | solution.py:989
  (127 shorter events, 14.9 us)
Async XLA Ops:
  0.6 6.5 %copy-start.12 = (f32[96]{0:T(128)S(1)}, f32[96]{0:T(128)}, u32[]{:S(2)}) copy-start(f32[96]{0:T(128)} %param.30) | copy-start | bytes 1156
  1.4 11.2 %collective-permute-start.2 = (bf16[3,16,512]{2,1,0:T(8,128)(2,1)S(1)}, bf16[3,16,512]{2,1,0:T(8,128)(2,1)S(1)}, u32[]{:S(2)}, u32[]{:S(2)}) collective-permute-start(bf16[3,16,512]{2,1,0:T(8,128)(2,1)S(1)} %pack_self.1), channel_id=1, source_target_pairs={{0,8},{1,9},{2,10},{3,11},{4,12},{5,13},{6,14},{7,15},{8,0},{9,1},... | collective-permute-start | bytes 147464 | tf_op jit(solution)/shard_map/ppermute | solution.py:989
  4.5 8.1 %collective-permute-start.1 = (bf16[3,16,512]{2,1,0:T(8,128)(2,1)S(1)}, bf16[3,16,512]{2,1,0:T(8,128)(2,1)S(1)}, u32[]{:S(2)}, u32[]{:S(2)}) collective-permute-start(bf16[3,16,512]{2,1,0:T(8,128)(2,1)S(1)} %pack_self.1), channel_id=1, source_target_pairs={{0,16},{1,17},{2,18},{3,19},{4,20},{5,21},{6,22},{7,23},{8,24},{9,... | collective-permute-start | bytes 147464 | tf_op jit(solution)/shard_map/ppermute | solution.py:989
  7.1 6.5 %collective-permute-start = (bf16[3,16,512]{2,1,0:T(8,128)(2,1)S(1)}, bf16[3,16,512]{2,1,0:T(8,128)(2,1)S(1)}, u32[]{:S(2)}, u32[]{:S(2)}) collective-permute-start(bf16[3,16,512]{2,1,0:T(8,128)(2,1)S(1)} %pack_self.1), channel_id=1, source_target_pairs={{0,24},{1,25},{2,26},{3,27},{4,28},{5,29},{6,30},{7,31},{8,16},{9,... | collective-permute-start | bytes 147464 | tf_op jit(solution)/shard_map/ppermute | solution.py:989
  8.6 11.2 %collective-permute-start.3 = (bf16[5,16,512]{2,1,0:T(8,128)(2,1)S(1)}, bf16[5,16,512]{2,1,0:T(8,128)(2,1)S(1)}, u32[]{:S(2)}, u32[]{:S(2)}) collective-permute-start(bf16[5,16,512]{2,1,0:T(8,128)(2,1)S(1)} %pack_cross.1), channel_id=1, source_target_pairs={{0,16},{1,17},{2,18},{3,19},{4,20},{5,21},{6,22},{7,23},{8,24},{9,... | collective-permute-start | bytes 245768 | tf_op jit(solution)/shard_map/ppermute | solution.py:989
  10.5 6.7 %copy-start.3 = (s32[1,16]{1,0:T(1,128)S(1)}, s32[1,16]{1,0:T(1,128)}, u32[]{:S(2)}) copy-start(s32[1,16]{1,0:T(1,128)} %seg_ref) | copy-start | bytes 196
  10.5 6.7 %copy-start.4 = (s32[1,17]{1,0:T(1,128)S(1)}, s32[1,17]{1,0:T(1,128)}, u32[]{:S(2)}) copy-start(s32[1,17]{1,0:T(1,128)} %mem_ref) | copy-start | bytes 208
  11.5 10.6 %collective-permute-start.12 = (bf16[144,512]{1,0:T(8,128)(2,1)S(1)}, bf16[144,512]{1,0:T(8,128)(2,1)S(1)}, u32[]{:S(2)}, u32[]{:S(2)}) collective-permute-start(bf16[144,512]{1,0:T(8,128)(2,1)S(1)} %bitcast.142), channel_id=1, source_target_pairs={{0,16},{1,17},{2,18},{3,19},{4,20},{5,21},{6,22},{7,23},{8,24},{9,... | collective-permute-start | bytes 442376 | tf_op jit(solution)/shard_map/ppermute | solution.py:989
  13.7 8.6 %collective-permute-start.10 = (bf16[3,4,16,512]{3,2,0,1:T(8,128)(2,1)S(1)}, bf16[3,4,16,512]{3,2,0,1:T(8,128)(2,1)S(1)}, u32[]{:S(2)}, u32[]{:S(2)}) collective-permute-start(bf16[3,4,16,512]{3,2,0,1:T(8,128)(2,1)S(1)} %pad_maximum_fusion.7), channel_id=1, source_target_pairs={{0,6},{1,7},{2,4},{3,5},{4,2},{5,3},{6,0},{7,1},{8,14},{9,15},{10,... | collective-permute-start | bytes 589832 | tf_op jit(solution)/shard_map/ppermute | solution.py:989
  16.2 7.2 %collective-permute-start.9 = (bf16[3,4,16,512]{3,2,0,1:T(8,128)(2,1)S(1)}, bf16[3,4,16,512]{3,2,0,1:T(8,128)(2,1)S(1)}, u32[]{:S(2)}, u32[]{:S(2)}) collective-permute-start(bf16[3,4,16,512]{3,2,0,1:T(8,128)(2,1)S(1)} %pad_maximum_fusion.7), channel_id=1, source_target_pairs={{0,4},{1,5},{2,6},{3,7},{4,0},{5,1},{6,2},{7,3},{8,12},{9,13},{10,... | collective-permute-start | bytes 589832 | tf_op jit(solution)/shard_map/ppermute | solution.py:989
  16.7 6.8 %collective-permute-start.8 = (bf16[3,4,16,512]{3,2,0,1:T(8,128)(2,1)S(1)}, bf16[3,4,16,512]{3,2,0,1:T(8,128)(2,1)S(1)}, u32[]{:S(2)}, u32[]{:S(2)}) collective-permute-start(bf16[3,4,16,512]{3,2,0,1:T(8,128)(2,1)S(1)} %pad_maximum_fusion.7), channel_id=1, source_target_pairs={{0,2},{1,3},{2,0},{3,1},{4,6},{5,7},{6,4},{7,5},{8,10},{9,11},{10,... | collective-permute-start | bytes 589832 | tf_op jit(solution)/shard_map/ppermute | solution.py:989
  19.8 6.6 %collective-permute-start.4 = (bf16[5,2,16,512]{3,2,1,0:T(8,128)(2,1)S(1)}, bf16[5,2,16,512]{3,2,1,0:T(8,128)(2,1)S(1)}, u32[]{:S(2)}, u32[]{:S(2)}) collective-permute-start(bf16[5,2,16,512]{3,2,1,0:T(8,128)(2,1)S(1)} %pad_maximum_fusion.8), channel_id=1, source_target_pairs={{0,8},{1,9},{2,10},{3,11},{4,12},{5,13},{6,14},{7,15},{8,0},{9,1},... | collective-permute-start | bytes 491528 | tf_op jit(solution)/shard_map/ppermute | solution.py:989
  22.2 9.4 %collective-permute-start.13 = (bf16[2,144,512]{2,1,0:T(8,128)(2,1)S(1)}, bf16[2,144,512]{2,1,0:T(8,128)(2,1)S(1)}, u32[]{:S(2)}, u32[]{:S(2)}) collective-permute-start(bf16[2,144,512]{2,1,0:T(8,128)(2,1)S(1)} %pad_maximum_fusion.5), channel_id=1, source_target_pairs={{0,8},{1,9},{2,10},{3,11},{4,12},{5,13},{6,14},{7,15},{8,0},{9,1},... | collective-permute-start | bytes 884744 | tf_op jit(solution)/shard_map/ppermute | solution.py:989
  23.8 7.9 %collective-permute-start.11 = (bf16[3,4,4,16,512]{4,3,0,1,2:T(8,128)(2,1)S(1)}, bf16[3,4,4,16,512]{4,3,0,1,2:T(8,128)(2,1)S(1)}, u32[]{:S(2)}, u32[]{:S(2)}) collective-permute-start(bf16[3,4,4,16,512]{4,3,0,1,2:T(8,128)(2,1)S(1)} %pad_maximum_fusion.3), channel_id=1, source_target_pairs={{0,1},{1,0},{2,3},{3,2},{4,5},{5,4},{6,7},{7,6},{8,9},{9,8},{10,11... | collective-permute-start | bytes 2359304 | tf_op jit(solution)/shard_map/ppermute | solution.py:989
  26.5 20.7 %collective-permute-start.7 = (bf16[5,2,2,16,512]{4,3,2,1,0:T(8,128)(2,1)S(1)}, bf16[5,2,2,16,512]{4,3,2,1,0:T(8,128)(2,1)S(1)}, u32[]{:S(2)}, u32[]{:S(2)}) collective-permute-start(bf16[5,2,2,16,512]{4,3,2,1,0:T(8,128)(2,1)S(1)} %pad_maximum_fusion.4.rest_0_), channel_id=1, source_target_pairs={{0,6},{1,7},{2,4},{3,5},{4,2},{5,3},{6,0},{7,1},{8,14},{9,15},{10,... | collective-permute-start | bytes 983048 | tf_op jit(solution)/shard_map/ppermute | solution.py:989
  29.0 18.2 %collective-permute-start.6 = (bf16[5,2,2,16,512]{4,3,2,1,0:T(8,128)(2,1)S(1)}, bf16[5,2,2,16,512]{4,3,2,1,0:T(8,128)(2,1)S(1)}, u32[]{:S(2)}, u32[]{:S(2)}) collective-permute-start(bf16[5,2,2,16,512]{4,3,2,1,0:T(8,128)(2,1)S(1)} %pad_maximum_fusion.4.rest_0_), channel_id=1, source_target_pairs={{0,4},{1,5},{2,6},{3,7},{4,0},{5,1},{6,2},{7,3},{8,12},{9,13},{10,... | collective-permute-start | bytes 983048 | tf_op jit(solution)/shard_map/ppermute | solution.py:989
  29.5 17.7 %collective-permute-start.5 = (bf16[5,2,2,16,512]{4,3,2,1,0:T(8,128)(2,1)S(1)}, bf16[5,2,2,16,512]{4,3,2,1,0:T(8,128)(2,1)S(1)}, u32[]{:S(2)}, u32[]{:S(2)}) collective-permute-start(bf16[5,2,2,16,512]{4,3,2,1,0:T(8,128)(2,1)S(1)} %pad_maximum_fusion.4.rest_0_), channel_id=1, source_target_pairs={{0,2},{1,3},{2,0},{3,1},{4,6},{5,7},{6,4},{7,5},{8,10},{9,11},{10,... | collective-permute-start | bytes 983048 | tf_op jit(solution)/shard_map/ppermute | solution.py:989
  32.1 15.1 %copy-start = (bf16[3,4,4,2,16,512]{5,4,3,2,1,0:T(8,128)(2,1)}, bf16[3,4,4,2,16,512]{5,4,3,2,1,0:T(8,128)(2,1)S(1)}, u32[]{:S(2)}) copy-start(bf16[3,4,4,2,16,512]{5,4,3,2,1,0:T(8,128)(2,1)S(1)} %copy.37) | copy-start | bytes 4718596
  32.1 15.5 %collective-permute-start.15 = (bf16[2,2,64,512]{3,2,1,0:T(8,128)(2,1)S(1)}, bf16[2,2,64,512]{3,2,1,0:T(8,128)(2,1)S(1)}, u32[]{:S(2)}, u32[]{:S(2)}) collective-permute-start(bf16[2,2,64,512]{3,2,1,0:T(8,128)(2,1)S(1)} %pad_maximum_fusion.6.rest_2_.refs_0_), channel_id=1, source_target_pairs={{0,4},{1,5},{2,6},{3,7},{4,0},{5,1},{6,2},{7,3},{8,12},{9,13},{10,... | collective-permute-start | bytes 786440 | tf_op jit(solution)/shard_map/ppermute | solution.py:989
  33.7 15.3 %collective-permute-start.14 = (bf16[2,2,80,512]{3,2,1,0:T(8,128)(2,1)S(1)}, bf16[2,2,80,512]{3,2,1,0:T(8,128)(2,1)S(1)}, u32[]{:S(2)}, u32[]{:S(2)}) collective-permute-start(bf16[2,2,80,512]{3,2,1,0:T(8,128)(2,1)S(1)} %fusion.1.rest_1_.refs_0_), channel_id=1, source_target_pairs={{0,2},{1,3},{2,0},{3,1},{4,6},{5,7},{6,4},{7,5},{8,10},{9,11},{10,... | collective-permute-start | bytes 983048 | tf_op jit(solution)/shard_map/ppermute | solution.py:989
  49.0 3.8 %collective-permute-start.16 = (bf16[5,2,2,4,16,512]{5,4,2,1,0,3:T(8,128)(2,1)S(1)}, bf16[5,2,2,4,16,512]{5,4,2,1,0,3:T(8,128)(2,1)}, u32[]{:S(2)}, u32[]{:S(2)}) collective-permute-start(bf16[5,2,2,4,16,512]{5,4,2,1,0,3:T(8,128)(2,1)S(1)} %pad_maximum_fusion.2), channel_id=1, source_target_pairs={{0,1},{1,0},{2,3},{3,2},{4,5},{5,4},{6,7},{7,6},{8,9},{9,8},{10,11... | collective-permute-start | bytes 3932168 | tf_op jit(solution)/shard_map/ppermute | solution.py:989
  49.9 23.9 %collective-permute-start.20 = (bf16[2,2,2,64,512]{4,3,2,1,0:T(8,128)(2,1)}, bf16[2,2,2,64,512]{4,3,2,1,0:T(8,128)(2,1)}, u32[]{:S(2)}, u32[]{:S(2)}) collective-permute-start(bf16[2,2,2,64,512]{4,3,2,1,0:T(8,128)(2,1)} %place.3), channel_id=1, source_target_pairs={{0,1},{1,0},{2,3},{3,2},{4,5},{5,4},{6,7},{7,6},{8,9},{9,8},{10,11... | collective-permute-start | bytes 1572872 | tf_op jit(solution)/shard_map/ppermute | solution.py:989
  50.4 23.4 %collective-permute-start.18 = (bf16[2,2,2,64,512]{4,3,2,1,0:T(8,128)(2,1)}, bf16[2,2,2,64,512]{4,3,2,1,0:T(8,128)(2,1)}, u32[]{:S(2)}, u32[]{:S(2)}) collective-permute-start(bf16[2,2,2,64,512]{4,3,2,1,0:T(8,128)(2,1)} %place.3), channel_id=1, source_target_pairs={{0,2},{1,3},{2,0},{3,1},{4,6},{5,7},{6,4},{7,5},{8,10},{9,11},{10,... | collective-permute-start | bytes 1572872 | tf_op jit(solution)/shard_map/ppermute | solution.py:989
  51.3 22.5 %collective-permute-start.19 = (bf16[2,2,2,80,512]{4,3,2,1,0:T(8,128)(2,1)S(1)}, bf16[2,2,2,80,512]{4,3,2,1,0:T(8,128)(2,1)}, u32[]{:S(2)}, u32[]{:S(2)}) collective-permute-start(bf16[2,2,2,80,512]{4,3,2,1,0:T(8,128)(2,1)S(1)} %place.2), channel_id=1, source_target_pairs={{0,1},{1,0},{2,3},{3,2},{4,5},{5,4},{6,7},{7,6},{8,9},{9,8},{10,11... | collective-permute-start | bytes 1966088 | tf_op jit(solution)/shard_map/ppermute | solution.py:989
  51.4 22.4 %collective-permute-start.17 = (bf16[2,2,2,80,512]{4,3,2,1,0:T(8,128)(2,1)S(1)}, bf16[2,2,2,80,512]{4,3,2,1,0:T(8,128)(2,1)}, u32[]{:S(2)}, u32[]{:S(2)}) collective-permute-start(bf16[2,2,2,80,512]{4,3,2,1,0:T(8,128)(2,1)S(1)} %place.2), channel_id=1, source_target_pairs={{0,4},{1,5},{2,6},{3,7},{4,0},{5,1},{6,2},{7,3},{8,12},{9,13},{10,... | collective-permute-start | bytes 1966088 | tf_op jit(solution)/shard_map/ppermute | solution.py:989
  73.8 3.1 %collective-permute-start.21 = (bf16[2,2,2,80,512]{4,3,2,1,0:T(8,128)(2,1)}, bf16[2,2,2,80,512]{4,3,2,1,0:T(8,128)(2,1)S(1)}, u32[]{:S(2)}, u32[]{:S(2)}) collective-permute-start(bf16[2,2,2,80,512]{4,3,2,1,0:T(8,128)(2,1)} %collective-permute-done.17), channel_id=1, source_target_pairs={{0,1},{1,0},{2,3},{3,2},{4,5},{5,4},{6,7},{7,6},{8,9},{9,8},{10,11... | collective-permute-start | bytes 1966088 | tf_op jit(solution)/shard_map/ppermute | solution.py:989
  74.1 2.9 %collective-permute-start.22 = (bf16[2,2,2,64,512]{4,3,2,1,0:T(8,128)(2,1)}, bf16[2,2,2,64,512]{4,3,2,1,0:T(8,128)(2,1)S(1)}, u32[]{:S(2)}, u32[]{:S(2)}) collective-permute-start(bf16[2,2,2,64,512]{4,3,2,1,0:T(8,128)(2,1)} %collective-permute-done.18), channel_id=1, source_target_pairs={{0,1},{1,0},{2,3},{3,2},{4,5},{5,4},{6,7},{7,6},{8,9},{9,8},{10,11... | collective-permute-start | bytes 1572872 | tf_op jit(solution)/shard_map/ppermute | solution.py:989
  103.9 9.1 %collective-permute-start.23 = (bf16[16,9,16,512]{3,2,1,0:T(8,128)(2,1)S(1)}, bf16[16,9,16,512]{3,2,1,0:T(8,128)(2,1)S(1)}, u32[]{:S(2)}, u32[]{:S(2)}) collective-permute-start(bf16[16,9,16,512]{3,2,1,0:T(8,128)(2,1)S(1)} %get-tuple-element.181), channel_id=1, source_target_pairs={{0,1},{1,0},{2,3},{3,2},{4,5},{5,4},{6,7},{7,6},{8,9},{9,8},{10,11... | collective-permute-start | bytes 7077896 | tf_op jit(solution)/shard_map/ppermute | solution.py:989
  114.2 21.3 %collective-permute-start.25 = (bf16[4,2,4,16,512]{4,3,2,1,0:T(8,128)(2,1)S(1)}, bf16[4,2,4,16,512]{4,3,2,1,0:T(8,128)(2,1)S(1)}, u32[]{:S(2)}, u32[]{:S(2)}) collective-permute-start(bf16[4,2,4,16,512]{4,3,2,1,0:T(8,128)(2,1)S(1)} %get-tuple-element.185.rest_1_), channel_id=1, source_target_pairs={{0,4},{1,5},{2,6},{3,7},{4,0},{5,1},{6,2},{7,3},{8,12},{9,13},{10,... | collective-permute-start | bytes 1572872 | tf_op jit(solution)/shard_map/ppermute | solution.py:989
  117.1 18.5 %collective-permute-start.24 = (bf16[4,2,5,16,512]{4,3,2,1,0:T(8,128)(2,1)S(1)}, bf16[4,2,5,16,512]{4,3,2,1,0:T(8,128)(2,1)S(1)}, u32[]{:S(2)}, u32[]{:S(2)}) collective-permute-start(bf16[4,2,5,16,512]{4,3,2,1,0:T(8,128)(2,1)S(1)} %get-tuple-element.184.rest_0_), channel_id=1, source_target_pairs={{0,2},{1,3},{2,0},{3,1},{4,6},{5,7},{6,4},{7,5},{8,10},{9,11},{10,... | collective-permute-start | bytes 1966088 | tf_op jit(solution)/shard_map/ppermute | solution.py:989
  136.5 13.7 %collective-permute-start.27 = (bf16[4,4,16,512]{3,2,1,0:T(8,128)(2,1)S(1)}, bf16[4,4,16,512]{3,2,1,0:T(8,128)(2,1)S(1)}, u32[]{:S(2)}, u32[]{:S(2)}) collective-permute-start(bf16[4,4,16,512]{3,2,1,0:T(8,128)(2,1)S(1)} %get-tuple-element.202.rest_1_), channel_id=1, source_target_pairs={{0,2},{1,3},{2,0},{3,1},{4,6},{5,7},{6,4},{7,5},{8,10},{9,11},{10,... | collective-permute-start | bytes 786440 | tf_op jit(solution)/shard_map/ppermute | solution.py:989
  140.0 10.3 %collective-permute-start.26 = (bf16[4,5,16,512]{3,2,1,0:T(8,128)(2,1)S(1)}, bf16[4,5,16,512]{3,2,1,0:T(8,128)(2,1)S(1)}, u32[]{:S(2)}, u32[]{:S(2)}) collective-permute-start(bf16[4,5,16,512]{3,2,1,0:T(8,128)(2,1)S(1)} %get-tuple-element.201.rest_0_), channel_id=1, source_target_pairs={{0,4},{1,5},{2,6},{3,7},{4,0},{5,1},{6,2},{7,3},{8,12},{9,13},{10,... | collective-permute-start | bytes 983048 | tf_op jit(solution)/shard_map/ppermute | solution.py:989
  150.4 3.1 %collective-permute-start.28 = (bf16[16,5,16,512]{3,2,1,0:T(8,128)(2,1)S(1)}, bf16[16,5,16,512]{3,2,1,0:T(8,128)(2,1)S(1)}, u32[]{:S(2)}, u32[]{:S(2)}) collective-permute-start(bf16[16,5,16,512]{3,2,1,0:T(8,128)(2,1)S(1)} %get-tuple-element.214), channel_id=1, source_target_pairs={{0,1},{1,0},{2,3},{3,2},{4,5},{5,4},{6,7},{7,6},{8,9},{9,8},{10,11... | collective-permute-start | bytes 3932168 | tf_op jit(solution)/shard_map/ppermute | solution.py:989
  150.5 23.0 %collective-permute-start.32 = (bf16[2,9,16,512]{3,2,1,0:T(8,128)(2,1)S(1)}, bf16[2,9,16,512]{3,2,1,0:T(8,128)(2,1)S(1)}, u32[]{:S(2)}, u32[]{:S(2)}) collective-permute-start(bf16[2,9,16,512]{3,2,1,0:T(8,128)(2,1)S(1)} %get-tuple-element.210.rest_0_), channel_id=1, source_target_pairs={{0,8},{1,9},{2,10},{3,11},{4,12},{5,13},{6,14},{7,15},{8,0},{9,1},... | collective-permute-start | bytes 884744 | tf_op jit(solution)/shard_map/ppermute | solution.py:989
  153.5 4.0 %copy-start.9 = (bf16[1024,512]{1,0:T(8,128)(2,1)S(1)}, bf16[1024,512]{1,0:T(8,128)(2,1)}, u32[]{:S(2)}) copy-start(bf16[1024,512]{1,0:T(8,128)(2,1)} %get-tuple-element.173.v_ref) | copy-start | bytes 3145732
  154.0 19.6 %collective-permute-start.29 = (bf16[4,5,16,512]{3,2,1,0:T(8,128)(2,1)S(1)}, bf16[4,5,16,512]{3,2,1,0:T(8,128)(2,1)S(1)}, u32[]{:S(2)}, u32[]{:S(2)}) collective-permute-start(bf16[4,5,16,512]{3,2,1,0:T(8,128)(2,1)S(1)} %get-tuple-element.215.rest_1_), channel_id=1, source_target_pairs={{0,2},{1,3},{2,0},{3,1},{4,6},{5,7},{6,4},{7,5},{8,10},{9,11},{10,... | collective-permute-start | bytes 983048 | tf_op jit(solution)/shard_map/ppermute | solution.py:989
  155.9 17.7 %collective-permute-start.30 = (bf16[4,5,16,512]{3,2,1,0:T(8,128)(2,1)S(1)}, bf16[4,5,16,512]{3,2,1,0:T(8,128)(2,1)S(1)}, u32[]{:S(2)}, u32[]{:S(2)}) collective-permute-start(bf16[4,5,16,512]{3,2,1,0:T(8,128)(2,1)S(1)} %get-tuple-element.216.rest_2_), channel_id=1, source_target_pairs={{0,4},{1,5},{2,6},{3,7},{4,0},{5,1},{6,2},{7,3},{8,12},{9,13},{10,... | collective-permute-start | bytes 983048 | tf_op jit(solution)/shard_map/ppermute | solution.py:989
  156.1 17.5 %collective-permute-start.31 = (bf16[4,5,16,512]{3,2,1,0:T(8,128)(2,1)S(1)}, bf16[4,5,16,512]{3,2,1,0:T(8,128)(2,1)S(1)}, u32[]{:S(2)}, u32[]{:S(2)}) collective-permute-start(bf16[4,5,16,512]{3,2,1,0:T(8,128)(2,1)S(1)} %get-tuple-element.217.rest_3_), channel_id=1, source_target_pairs={{0,6},{1,7},{2,4},{3,5},{4,2},{5,3},{6,0},{7,1},{8,14},{9,15},{10,... | collective-permute-start | bytes 983048 | tf_op jit(solution)/shard_map/ppermute | solution.py:989
  173.8 4.2 %collective-permute-start.33 = (bf16[16,3,16,512]{3,2,1,0:T(8,128)(2,1)S(1)}, bf16[16,3,16,512]{3,2,1,0:T(8,128)(2,1)S(1)}, u32[]{:S(2)}, u32[]{:S(2)}) collective-permute-start(bf16[16,3,16,512]{3,2,1,0:T(8,128)(2,1)S(1)} %get-tuple-element.230), channel_id=1, source_target_pairs={{0,1},{1,0},{2,3},{3,2},{4,5},{5,4},{6,7},{7,6},{8,9},{9,8},{10,11... | collective-permute-start | bytes 2359304 | tf_op jit(solution)/shard_map/ppermute | solution.py:989
  173.9 13.6 %collective-permute-start.42 = (bf16[1,9,16,512]{3,2,1,0:T(8,128)(2,1)S(1)}, bf16[1,9,16,512]{3,2,1,0:T(8,128)(2,1)S(1)}, u32[]{:S(2)}, u32[]{:S(2)}) collective-permute-start(bf16[1,9,16,512]{3,2,1,0:T(8,128)(2,1)S(1)} %get-tuple-element.228), channel_id=1, source_target_pairs={{0,16},{1,17},{2,18},{3,19},{4,20},{5,21},{6,22},{7,23},{8,24},{9,... | collective-permute-start | bytes 442376 | tf_op jit(solution)/shard_map/ppermute | solution.py:989
  175.2 9.4 %collective-permute-start.40 = (bf16[2,5,16,512]{3,2,1,0:T(8,128)(2,1)S(1)}, bf16[2,5,16,512]{3,2,1,0:T(8,128)(2,1)S(1)}, u32[]{:S(2)}, u32[]{:S(2)}) collective-permute-start(bf16[2,5,16,512]{3,2,1,0:T(8,128)(2,1)S(1)} %get-tuple-element.225), channel_id=1, source_target_pairs={{0,8},{1,9},{2,10},{3,11},{4,12},{5,13},{6,14},{7,15},{8,0},{9,1},... | collective-permute-start | bytes 491528 | tf_op jit(solution)/shard_map/ppermute | solution.py:989
  178.2 11.0 %collective-permute-start.35 = (bf16[4,3,16,512]{3,2,1,0:T(8,128)(2,1)S(1)}, bf16[4,3,16,512]{3,2,1,0:T(8,128)(2,1)S(1)}, u32[]{:S(2)}, u32[]{:S(2)}) collective-permute-start(bf16[4,3,16,512]{3,2,1,0:T(8,128)(2,1)S(1)} %get-tuple-element.233), channel_id=1, source_target_pairs={{0,4},{1,5},{2,6},{3,7},{4,0},{5,1},{6,2},{7,3},{8,12},{9,13},{10,... | collective-permute-start | bytes 589832 | tf_op jit(solution)/shard_map/ppermute | solution.py:989
  179.7 9.5 %collective-permute-start.36 = (bf16[4,3,16,512]{3,2,1,0:T(8,128)(2,1)S(1)}, bf16[4,3,16,512]{3,2,1,0:T(8,128)(2,1)S(1)}, u32[]{:S(2)}, u32[]{:S(2)}) collective-permute-start(bf16[4,3,16,512]{3,2,1,0:T(8,128)(2,1)S(1)} %get-tuple-element.234), channel_id=1, source_target_pairs={{0,6},{1,7},{2,4},{3,5},{4,2},{5,3},{6,0},{7,1},{8,14},{9,15},{10,... | collective-permute-start | bytes 589832 | tf_op jit(solution)/shard_map/ppermute | solution.py:989
  180.3 10.1 %collective-permute-start.34 = (bf16[4,3,16,512]{3,2,1,0:T(8,128)(2,1)S(1)}, bf16[4,3,16,512]{3,2,1,0:T(8,128)(2,1)S(1)}, u32[]{:S(2)}, u32[]{:S(2)}) collective-permute-start(bf16[4,3,16,512]{3,2,1,0:T(8,128)(2,1)S(1)} %get-tuple-element.232), channel_id=1, source_target_pairs={{0,2},{1,3},{2,0},{3,1},{4,6},{5,7},{6,4},{7,5},{8,10},{9,11},{10,... | collective-permute-start | bytes 589832 | tf_op jit(solution)/shard_map/ppermute | solution.py:989
  184.6 7.2 %collective-permute-start.41 = (bf16[1,5,16,512]{3,2,1,0:T(8,128)(2,1)S(1)}, bf16[1,5,16,512]{3,2,1,0:T(8,128)(2,1)S(1)}, u32[]{:S(2)}, u32[]{:S(2)}) collective-permute-start(bf16[1,5,16,512]{3,2,1,0:T(8,128)(2,1)S(1)} %get-tuple-element.244), channel_id=1, source_target_pairs={{0,16},{1,17},{2,18},{3,19},{4,20},{5,21},{6,22},{7,23},{8,24},{9,... | collective-permute-start | bytes 245768 | tf_op jit(solution)/shard_map/ppermute | solution.py:989
  190.5 8.5 %collective-permute-start.37 = (bf16[1,3,16,512]{3,2,1,0:T(8,128)(2,1)S(1)}, bf16[1,3,16,512]{3,2,1,0:T(8,128)(2,1)S(1)}, u32[]{:S(2)}, u32[]{:S(2)}) collective-permute-start(bf16[1,3,16,512]{3,2,1,0:T(8,128)(2,1)S(1)} %get-tuple-element.236), channel_id=1, source_target_pairs={{0,8},{1,9},{2,10},{3,11},{4,12},{5,13},{6,14},{7,15},{8,0},{9,1},... | collective-permute-start | bytes 147464 | tf_op jit(solution)/shard_map/ppermute | solution.py:989
  191.8 6.6 %collective-permute-start.38 = (bf16[1,3,16,512]{3,2,1,0:T(8,128)(2,1)S(1)}, bf16[1,3,16,512]{3,2,1,0:T(8,128)(2,1)S(1)}, u32[]{:S(2)}, u32[]{:S(2)}) collective-permute-start(bf16[1,3,16,512]{3,2,1,0:T(8,128)(2,1)S(1)} %get-tuple-element.237), channel_id=1, source_target_pairs={{0,16},{1,17},{2,18},{3,19},{4,20},{5,21},{6,22},{7,23},{8,24},{9,... | collective-permute-start | bytes 147464 | tf_op jit(solution)/shard_map/ppermute | solution.py:989
  193.1 5.9 %collective-permute-start.39 = (bf16[1,3,16,512]{3,2,1,0:T(8,128)(2,1)S(1)}, bf16[1,3,16,512]{3,2,1,0:T(8,128)(2,1)S(1)}, u32[]{:S(2)}, u32[]{:S(2)}) collective-permute-start(bf16[1,3,16,512]{3,2,1,0:T(8,128)(2,1)S(1)} %get-tuple-element.238), channel_id=1, source_target_pairs={{0,24},{1,25},{2,26},{3,27},{4,28},{5,29},{6,30},{7,31},{8,16},{9,... | collective-permute-start | bytes 147464 | tf_op jit(solution)/shard_map/ppermute | solution.py:989
  (8 other events, 30.7 us)
